TPU v7x, 512 devices: a whole 4x4x16 slice. The times are simulated.
512 devices in a mesh: lon: 64 (over x, z_hi, y, core), lat: 8 (over z_lo).
Axes of the slice: x: 4, y: 4, z: 16 (z_hi: 2, z_lo: 8; z = z_hi * 8 + z_lo), core: 2. Of those that a mesh axis runs over, the one named last changes fastest.
Arguments:
- latent_field: bfloat16 [2, 48, 768, 384], P(None, 'lat', 'lon'), may hold values from -6 to 6
- cotangent: bfloat16 [2, 48, 768, 384], P(None, 'lat', 'lon'), may hold values from -16 to 16
- norm_gain: float32 [384], replicated, may hold values from 0.1 to 1.9
- input_weight: bfloat16 [384, 1152], replicated, may hold values from -0.3125 to 0.3125
- output_weight: bfloat16 [384, 384], replicated, may hold values from -0.3125 to 0.3125
- bias_table: bfloat16 [8, 12, 3312], P('lat'), may hold values from -6 to 256
- regions: int32 [2, 48, 768], P(None, 'lat', 'lon'), may hold values from 0 to 3
Outputs:
- grad_field: bfloat16 [2, 48, 768, 384], P(None, 'lat', 'lon')
- grad_input_weight: bfloat16 [384, 1152], P('lon')
- grad_output_weight: bfloat16 [384, 384], P('lon')
- grad_gain: float32 [384], replicated
- grad_table: float32 [8, 12, 3312], P('lat')
Inputs may be any that keep to these rules, and one draw needn't show every extreme that they name: `regions`: two cells of a window attend to each other only where their region ids agree.
All inputs are finite; a program needn't handle non-finite values.
Results may differ from a plain program's by a relative error of at most 0.02.
Values may be sent and summed in bfloat16 or wider, within the bound.
A program may use at most 128 MiB of HBM per device.

v0:
```python
import math

import jax
import jax.numpy as jnp
from jax import lax
from jax.sharding import PartitionSpec as P

HEADS = 12
LEV = 2
WIN_LAT = 6
WIN_LON = 12


norm_eps = 1e-05
masked_score = -1000000000.0
highest = lax.Precision.HIGHEST


def from_behind(value, axis, steps):
    count = lax.axis_size(axis)
    pairs = [(source, (source + steps) % count) for source in range(count)]
    return lax.ppermute(value, axis, pairs)


def longitude_onehot(span_cells):
    first_index = jnp.arange(span_cells)[:, None, None]
    second_index = jnp.arange(span_cells)[None, :, None]
    offset_index = jnp.arange(2 * span_cells - 1)[None, None, :]
    return (first_index - second_index + span_cells - 1 == offset_index).astype(jnp.float32)


def expand_bias(bias_rows):
    num_bands, num_heads = (bias_rows.shape[0], bias_rows.shape[1])
    shaped = bias_rows.astype(jnp.float32).reshape(
        num_bands, num_heads, LEV, LEV, WIN_LAT, WIN_LAT, 2 * WIN_LON - 1
    )
    spread = jnp.einsum(
        "bhxyuvr,cdr->bhxucyvd", shaped, longitude_onehot(WIN_LON), precision=highest
    )
    window_cells = LEV * WIN_LAT * WIN_LON
    return spread.reshape(num_bands, num_heads, window_cells, window_cells)


def fold_bias(grad_full):
    num_bands, num_heads = (grad_full.shape[0], grad_full.shape[1])
    shaped = grad_full.reshape(num_bands, num_heads, LEV, WIN_LAT, WIN_LON, LEV, WIN_LAT, WIN_LON)
    folded = jnp.einsum(
        "bhxucyvd,cdr->bhxyuvr", shaped, longitude_onehot(WIN_LON), precision=highest
    )
    return folded.reshape(num_bands, num_heads, -1)


def to_windows(cells_grid):
    levels, row_count, col_count = (cells_grid.shape[0], cells_grid.shape[1], cells_grid.shape[2])
    trailing = cells_grid.shape[3:]
    shaped = cells_grid.reshape(
        (levels, row_count // WIN_LAT, WIN_LAT, col_count // WIN_LON, WIN_LON) + trailing
    )
    axes_order = (1, 3, 0, 2, 4) + tuple(range(5, 5 + len(trailing)))
    return jnp.transpose(shaped, axes_order).reshape(
        (row_count // WIN_LAT, col_count // WIN_LON, levels * WIN_LAT * WIN_LON) + trailing
    )


def from_windows(blocks):
    num_bands, num_windows, features = (blocks.shape[0], blocks.shape[1], blocks.shape[3])
    shaped = blocks.reshape(num_bands, num_windows, LEV, WIN_LAT, WIN_LON, features)
    return jnp.transpose(shaped, (2, 0, 3, 1, 4, 5)).reshape(
        LEV, num_bands * WIN_LAT, num_windows * WIN_LON, features
    )


def window_grads(normed_win, grad_win, region_win, bias_rows, input_weight, output_weight):
    num_bands, num_windows, window_cells, features = normed_win.shape
    head_dim = features // HEADS
    score_scale = head_dim ** (-0.5)
    flat_normed = normed_win.reshape(-1, features)
    projected = jnp.dot(flat_normed, input_weight, preferred_element_type=jnp.float32).astype(
        jnp.bfloat16
    )
    projected = projected.reshape(num_bands, num_windows, window_cells, 3, HEADS, head_dim)
    queries, key_rows, values = (
        projected[:, :, :, 0],
        projected[:, :, :, 1],
        projected[:, :, :, 2],
    )
    scores = (
        jnp.einsum("bwihe,bwjhe->bwhij", queries, key_rows, preferred_element_type=jnp.float32)
        * score_scale
    )
    scores = scores + expand_bias(bias_rows)[:, None]
    same_region = region_win[:, :, :, None] == region_win[:, :, None, :]
    scores = jnp.where(same_region[:, :, None], scores, masked_score)
    softmax_out = jax.nn.softmax(scores, axis=-1)
    probs_low = softmax_out.astype(jnp.bfloat16)
    attended = jnp.einsum(
        "bwhij,bwjhe->bwihe", probs_low, values, preferred_element_type=jnp.float32
    ).astype(jnp.bfloat16)
    flat_attended = attended.reshape(-1, features)
    flat_grad = grad_win.reshape(-1, features)
    grad_attended = jnp.dot(flat_grad, output_weight.T, preferred_element_type=jnp.float32).astype(
        jnp.bfloat16
    )
    grad_attended = grad_attended.reshape(num_bands, num_windows, window_cells, HEADS, head_dim)
    grad_probs = jnp.einsum(
        "bwihe,bwjhe->bwhij", grad_attended, values, preferred_element_type=jnp.float32
    )
    grad_values = jnp.einsum(
        "bwhij,bwihe->bwjhe", probs_low, grad_attended, preferred_element_type=jnp.float32
    )
    grad_scores = softmax_out * (
        grad_probs - jnp.sum(softmax_out * grad_probs, axis=-1, keepdims=True)
    )
    grad_table = fold_bias(jnp.sum(grad_scores, axis=1))
    scores_low = (grad_scores * score_scale).astype(jnp.bfloat16)
    grad_queries = jnp.einsum(
        "bwhij,bwjhe->bwihe", scores_low, key_rows, preferred_element_type=jnp.float32
    )
    grad_keys = jnp.einsum(
        "bwhij,bwihe->bwjhe", scores_low, queries, preferred_element_type=jnp.float32
    )
    grad_projected = jnp.stack([grad_queries, grad_keys, grad_values], axis=3).astype(jnp.bfloat16)
    grad_projected = grad_projected.reshape(-1, 3 * features)
    grad_normed = jnp.dot(
        grad_projected, input_weight.T, preferred_element_type=jnp.float32
    ).astype(jnp.bfloat16)
    return (
        grad_normed.reshape(normed_win.shape),
        flat_normed,
        grad_projected,
        flat_attended,
        flat_grad,
        grad_table,
    )


def advance_longitude(stacked):
    half_cols = WIN_LON // 2
    edge_cells = from_behind(stacked[:, :, :, :half_cols], "lon", -1)
    return jnp.concatenate([stacked[:, :, :, half_cols:], edge_cells], axis=3)


def advance_latitude(stacked):
    half_rows = WIN_LAT // 2
    edge_cells = from_behind(stacked[:, :, :half_rows], "lat", -1)
    return jnp.concatenate([stacked[:, :, half_rows:], edge_cells], axis=2)


def retreat_longitude(cells_grid):
    half_cols = WIN_LON // 2
    edge_cells = from_behind(cells_grid[:, :, -half_cols:], "lon", 1)
    return jnp.concatenate([edge_cells, cells_grid[:, :, :-half_cols]], axis=2)


def retreat_latitude(cells_grid):
    half_rows = WIN_LAT // 2
    edge_cells = from_behind(cells_grid[:, -half_rows:], "lat", 1)
    return jnp.concatenate([edge_cells, cells_grid[:, :-half_rows]], axis=1)


def on_device(latent_field, cotangent, norm_gain, input_weight, output_weight, bias_table, regions):
    field_f32 = latent_field.astype(jnp.float32)
    centred = field_f32 - jnp.mean(field_f32, axis=-1, keepdims=True)
    inv_std = lax.rsqrt(jnp.mean(centred * centred, axis=-1, keepdims=True) + norm_eps)
    normalized = centred * inv_std
    normed = (normalized * norm_gain).astype(jnp.bfloat16)
    stacked = jnp.roll(jnp.stack([normed, cotangent]), -(LEV // 2), axis=1)
    stacked = advance_latitude(advance_longitude(stacked))
    features = latent_field.shape[3]

    def one_band(band_item):
        normed_band, grad_band, region_band, table_band = band_item
        return window_grads(
            normed_band[None],
            grad_band[None],
            region_band[None],
            table_band[None],
            input_weight,
            output_weight,
        )

    results = lax.map(
        one_band, (to_windows(stacked[0]), to_windows(stacked[1]), to_windows(regions), bias_table)
    )
    grad_windows, flat_normed, grad_projected, flat_attended, flat_grad, grad_table = results
    grad_windows = grad_windows[:, 0]
    grad_table = grad_table[:, 0]
    flat_normed = flat_normed.reshape(-1, features)
    grad_projected = grad_projected.reshape(-1, 3 * features)
    flat_attended = flat_attended.reshape(-1, features)
    flat_grad = flat_grad.reshape(-1, features)
    grad_shifted = from_windows(grad_windows)
    grad_back = retreat_latitude(retreat_longitude(grad_shifted))
    grad_normed = jnp.roll(grad_back, LEV // 2, axis=0)
    grad_f32 = grad_normed.astype(jnp.float32)
    scaled = grad_f32 * norm_gain
    grad_field = cotangent.astype(jnp.float32) + inv_std * (
        scaled
        - jnp.mean(scaled, axis=-1, keepdims=True)
        - normalized * jnp.mean(scaled * normalized, axis=-1, keepdims=True)
    )
    grad_gain = jnp.sum(grad_f32 * normalized, axis=(0, 1, 2))
    grad_gain, grad_table = lax.psum((grad_gain, grad_table), "lon")
    joined = jnp.concatenate(
        [
            jnp.dot(flat_normed.T, grad_projected, preferred_element_type=jnp.float32),
            jnp.dot(flat_attended.T, flat_grad, preferred_element_type=jnp.float32),
        ],
        axis=1,
    )
    joined, grad_gain = (
        lax.psum(joined.astype(jnp.bfloat16), "lat").astype(jnp.float32),
        lax.psum(grad_gain.astype(jnp.bfloat16), "lat").astype(jnp.float32),
    )
    shares = lax.psum_scatter(joined, "lon", scatter_dimension=0, tiled=True)
    total_cells = (
        latent_field.shape[0]
        * latent_field.shape[1]
        * latent_field.shape[2]
        * lax.axis_size("lon")
        * lax.axis_size("lat")
    )
    factor = 1.0 / math.sqrt(total_cells)
    grad_input_weight = (shares[:, : 3 * features] * factor).astype(jnp.bfloat16)
    grad_output_weight = (shares[:, 3 * features :] * factor).astype(jnp.bfloat16)
    return (
        grad_field.astype(jnp.bfloat16),
        grad_input_weight,
        grad_output_weight,
        grad_gain * factor,
        grad_table,
    )


def solution(mesh):
    in_specs = (
        P(None, "lat", "lon", None),
        P(None, "lat", "lon", None),
        P(),
        P(),
        P(),
        P("lat", None, None),
        P(None, "lat", "lon"),
    )
    out_specs = (
        P(None, "lat", "lon", None),
        P("lon", None),
        P("lon", None),
        P(),
        P("lat", None, None),
    )
    return jax.shard_map(
        on_device, mesh=mesh, in_specs=in_specs, out_specs=out_specs, check_vma=False
    )
```

profile of v0, /device:TPU:1, one launch (start us, length us, event | category | flops | bytes accessed | tf_op | source)
XLA Modules:
  0.0 1262.9 jit_solution(13096487709094703112)
XLA Ops:
  11.6 8.8 collective-permute-start
  21.5 10.4 collective-permute-start.1
  32.0 7.2 convolution_bitcast_fusion
  39.2 21.6 %copy.71 = f32[1,12,2,6,12,2,6,12]{4,3,2,7,6,5,1,0:T(8,128)} copy(f32[1,12,2,6,12,2,6,12]{1,7,6,3,5,2,4,0:T(8,128)} %convolution_bitcast_fusion) | data formatting | bytes 1990656 | tf_op jit(solution)/shard_map/while/body/eval_jaxpr/broadcast_in_dim;while/body/eval_jaxpr/reshape | solution.py:91
  60.7 10.3 reshape.295
  74.8 2.0 add_select_fusion
  76.8 1.6 fusion.55
  78.3 1.7 fusion.25
  80.0 2.1 convolution_bitcast_fusion.2
  82.1 4.4 convolution_bitcast_fusion.3
  86.5 4.4 convolution_bitcast_fusion.4
  94.4 2.0 collective-permute-start.2
  98.6 3.6 subtract_multiply_fusion
  102.2 10.1 reshape.296
  112.4 20.8 %copy.60 = f32[12,2,6,12,2,6,12]{6,0,3,5,4,2,1:T(8,128)} copy(f32[12,2,6,12,2,6,12]{3,2,1,6,5,4,0:T(8,128)} %reshape.296) | data formatting | bytes 1990656 | tf_op jit(solution)/shard_map/reshape.74
  133.2 1.9 collective-permute-start.3
  135.1 13.0 %convolution_bitcast_fusion.1 = f32[1,12,2,2,6,6,23]{6,1,5,3,4,2,0:T(8,128)S(1)} fusion(f32[12,2,6,12,2,6,12]{6,0,3,5,4,2,1:T(8,128)} %copy.60, s32[12,12]{1,0:T(8,128)S(1)} %subtract_add_fusion), kind=kOutput, calls=%fused_computation.11 | convolution fusion | flops 68680944 | bytes 1154880 | tf_op jit(solution)/shard_map/while/body/eval_jaxpr/bhxucyvd,cdr->bhxyuvr/dot_general | solution.py:47
  148.4 1.4 squeeze.19
  151.2 82.4 %all-reduce.6.cloned.1.call-done = bf16[384,1536]{1,0:T(8,128)(2,1)} async-done(((bf16[384,1536]{1,0:T(8,128)(2,1)}), bf16[384,1536]{1,0:T(8,128)(2,1)}) %all-reduce.6.cloned.1.call-update) | async-done | bytes 1179664 | tf_op jit(solution)/shard_map/psum | solution.py:212
  233.6 583.1 %all-reduce.9 = (f32[384,1536]{1,0:T(8,128)}, bf16[384]{0:T(512)(128)(2,1)S(1)}) all-reduce(bf16[384,1536]{1,0:T(8,128)(2,1)} %all-reduce.6.cloned.1.call-done, f32[384]{0:T(512)S(1)} %get-tuple-element.54), channel_id=2, replica_groups=mesh['lon'=64,'lat'=8] {'lon'}, use_global_device_ids=true, to_apply=%region_8.9.clone | all-reduce | flops 590208 | bytes 3541248
  816.7 26.6 %psum.30 = bf16[384]{0:T(512)(128)(2,1)S(1)} all-reduce(bf16[384]{0:T(512)(128)(2,1)S(1)} %get-tuple-element.58), channel_id=1, replica_groups=mesh['lon'=64,'lat'=8] {'lat'}, use_global_device_ids=true, to_apply=%region_11.12 | all-reduce | flops 384 | bytes 1536 | tf_op jit(solution)/shard_map/psum | solution.py:213
  843.3 1.5 fusion.46
  846.8 407.6 %all-reduce.8.cloned.1.call-done = f32[1,12,3312]{2,0,1:T(1,128)} async-done(((f32[1,12,3312]{2,0,1:T(1,128)}), f32[1,12,3312]{2,0,1:T(1,128)}) %all-reduce.8.cloned.1.call-update) | async-done | bytes 158992 | tf_op jit(solution)/shard_map/psum | solution.py:203
  1254.4 1.6 copy.96
  (71 shorter events, 17.7 us)
Async XLA Ops:
  7.2 67.0 %copy-start = (bf16[384,1152]{1,0:T(8,128)(2,1)S(1)}, bf16[384,1152]{1,0:T(8,128)(2,1)}, u32[]{:S(2)}) copy-start(bf16[384,1152]{1,0:T(8,128)(2,1)} %param.10) | copy-start | bytes 2654212
  7.2 13.2 %copy-start.8 = (bf16[1,12,3312]{2,1,0:T(8,128)(2,1)S(1)}, bf16[1,12,3312]{2,1,0:T(8,128)(2,1)}, u32[]{:S(2)}) copy-start(bf16[1,12,3312]{2,1,0:T(8,128)(2,1)} %param.12) | copy-start | bytes 238468
  7.2 14.0 %copy-start.10 = (s32[2,6,12]{2,0,1:T(2,128)S(1)}, s32[2,6,12]{2,0,1:T(2,128)}, u32[]{:S(2)}) copy-start(s32[2,6,12]{2,0,1:T(2,128)} %param.13) | copy-start | bytes 1732
  7.2 226.4 %all-reduce.6.cloned.1.call-start = ((), (), s32[]{:S(2)}) async-start(), calls=%async_computation | async-start | bytes 2359296 | tf_op jit(solution)/shard_map/psum | solution.py:212
  11.6 9.9 collective-permute-start
  21.5 51.4 %collective-permute-start.1 = (bf16[2,2,3,12,384]{4,3,2,1,0:T(8,128)(2,1)S(1)}, bf16[2,2,3,12,384]{4,3,2,1,0:T(8,128)(2,1)S(1)}, u32[]{:S(2)}, u32[]{:S(2)}) collective-permute-start(bf16[2,2,3,12,384]{4,3,2,1,0:T(8,128)(2,1)S(1)} %get-tuple-element.62), channel_id=1, source_target_pairs={{0,7},{1,0},{2,1},{3,2},{4,3},{5,4},{6,5},{7,6},{8,15},{9,8},{10,9... | collective-permute-start | bytes 331784 | tf_op jit(solution)/shard_map/ppermute | solution.py:22
  60.7 12.3 copy-start.6
  76.8 1.6 copy-start.4
  93.4 3.1 copy-start.7
  94.4 38.7 %collective-permute-start.2 = (bf16[2,6,6,384]{3,2,1,0:T(8,128)(2,1)S(1)}, bf16[2,6,6,384]{3,2,1,0:T(8,128)(2,1)S(1)}, u32[]{:S(2)}, u32[]{:S(2)}) collective-permute-start(bf16[2,6,6,384]{3,2,1,0:T(8,128)(2,1)S(1)} %get-tuple-element.67), channel_id=1, source_target_pairs={{0,8},{8,16},{16,24},{24,32},{32,40},{40,48},{48,56},{56,64},{64,7... | collective-permute-start | bytes 165896 | tf_op jit(solution)/shard_map/ppermute | solution.py:22
  96.7 1.9 copy-start.3
  97.9 1156.5 %all-reduce.8.cloned.1.call-start = ((), (), s32[]{:S(2)}) async-start(), calls=%async_computation.1 | async-start | bytes 319488 | tf_op jit(solution)/shard_map/psum | solution.py:203
  133.2 16.7 %collective-permute-start.3 = (bf16[2,3,12,384]{3,2,1,0:T(8,128)(2,1)S(1)}, bf16[2,3,12,384]{3,2,1,0:T(8,128)(2,1)S(1)}, u32[]{:S(2)}, u32[]{:S(2)}) collective-permute-start(bf16[2,3,12,384]{3,2,1,0:T(8,128)(2,1)S(1)} %fusion.43), channel_id=1, source_target_pairs={{0,1},{1,2},{2,3},{3,4},{4,5},{5,6},{6,7},{7,0},{8,9},{9,10},{10,1... | collective-permute-start | bytes 165896 | tf_op jit(solution)/shard_map/ppermute | solution.py:22
  148.1 1.9 copy-start.2
  148.1 1.9 copy-start.9
  148.4 1.8 copy-start.5
  149.9 1106.2 %copy-start.1 = (bf16[384,1152]{1,0:T(8,128)(2,1)S(1)}, bf16[384,1152]{1,0:T(8,128)(2,1)}, u32[]{:S(2)}) copy-start(bf16[384,1152]{1,0:T(8,128)(2,1)} %param.10) | copy-start | bytes 2654212
Sparse Core Ops, SparseCore 0:
  98.1 135.5 all-reduce.5
  237.1 1017.2 all-reduce.7
where the time goes:
time: 1260 us
  blocking collectives  610 us (48%)
  waiting for transfers between devices  490 us (39%)
  local copies, waits for them, and re-layouts  71.6 us (6%)
  matrix products  37.8 us (3%)
  starting transfers between devices  23.4 us (2%)
  other arithmetic  15.2 us (1%)
  between operations  15.1 us (1%)
    unnamed x1, blocking collectives  583 us
    psum x1, waiting for transfers between devices, on_device(): grad_gain, grad_table = lax.psum((grad_gain, grad_table), 'lon')  408 us
    psum x1, waiting for transfers between devices, on_device(): lax.psum(joined.astype(jnp.bfloat16), 'lat').astype(jnp.float32)  82.4 us
    reshape x2, local copies, waits for them, and re-layouts, window_grads(): scores = scores + expand_bias(bias_rows)[:, None]  31.9 us
    another operation x3, local copies, waits for them, and re-layouts  31.7 us
    psum x1, blocking collectives, on_device(): lax.psum(grad_gain.astype(jnp.bfloat16), 'lat').astype(jnp.float32)  26.6 us
  transfers between devices with their start and end apart: 6, of which 2 were waited for; matrix products, arithmetic and copies ran while one was open for 8% of the time, Pallas kernels for 0%

commit v1 on v0

v1 whole, which is shorter than its diff:
```python
import functools
import math

import jax
import jax.numpy as jnp
import numpy as np
from jax import lax
from jax.experimental import pallas as pl
from jax.experimental.pallas import tpu as pltpu
from jax.sharding import PartitionSpec as P

D = 384
HEADS = 12
HEAD_DIM = 32
LEV = 2
WIN_LAT = 6
WIN_LON = 12
CELLS = 144
ROWS = LEV * WIN_LAT
QUAD = 36
SLOT = 80
BACK = 48
SPREAD = 2 * WIN_LON - 1
HALF_POS = WIN_LAT * SPREAD
POS = 3312
WIDE = 256
CHUNK = 10
CHIPS = 16
CORE_TILES = 16
GAIN_TILE = 26
SCATTER = WIN_LON * ROWS * 16

norm_eps = 1e-05
masked_score = -1000000000.0
VMEM = pltpu.VMEM
f32 = jnp.float32
bf16 = jnp.bfloat16


def quad_of(p):
    lon, lev, lat = p // ROWS, (p % ROWS) // WIN_LAT, p % WIN_LAT
    quad = (lat // 3) * 2 + lon // 6
    return quad, (lev * 3 + lat % 3) * 6 + lon % 6


def gather_matrices():
    field = np.zeros((CELLS, 4 * SLOT), np.float32)
    cot = np.zeros((CELLS, 4 * SLOT), np.float32)
    back = np.zeros((4 * BACK, CELLS), np.float32)
    for p in range(CELLS):
        quad, place = quad_of(p)
        field[p, quad * SLOT + place] = 1
        cot[p, quad * SLOT + QUAD + place] = 1
        back[quad * BACK + place, p] = 1
    return field, cot, back


def feature_order():
    out = np.zeros((D, D), np.float32)
    r = 0
    for core in range(2):
        for x in range(4):
            for z_hi in range(2):
                for y in range(4):
                    lon = ((x * 2 + z_hi) * 4 + y) * 2 + core
                    for k in range(6):
                        out[r, lon * 6 + k] = 1
                        r += 1
    return out


def bias_selectors():
    out = np.zeros((WIN_LON, 2 * HALF_POS, WIDE), np.float32)
    for c in range(WIN_LON):
        for p in range(CELLS):
            d, yv = p // ROWS, p % ROWS
            out[c, (yv // WIN_LAT) * HALF_POS + (yv % WIN_LAT) * SPREAD + c - d + WIN_LON - 1, p] = 1
    return out


def head_rows(ref, h):
    return jnp.concatenate(
        [ref[pl.ds(half * SCATTER + h, CELLS, stride=16), :] for half in range(2)], axis=1
    )


def put_head_rows(ref, h, value):
    for half in range(2):
        ref[pl.ds(half * SCATTER + h, CELLS, stride=16), :] = value[:, half * 128 : half * 128 + 128]


def nt(a, b):
    return lax.dot_general(a, b, (((1,), (1,)), ((), ())), preferred_element_type=f32)


def nn(a, b):
    return lax.dot_general(a, b, (((1,), (0,)), ((), ())), preferred_element_type=f32)


def tn(a, b):
    return lax.dot_general(a, b, (((0,), (0,)), ((), ())), preferred_element_type=f32)


def iota(shape, dim):
    return lax.broadcasted_iota(jnp.int32, shape, dim)


def expand_table(table_ref, sel_ref, tprime, bias):
    table = table_ref[0].astype(f32)
    tprime[...] = jnp.zeros_like(tprime)
    for xu in range(ROWS):
        x, u = xu // WIN_LAT, xu % WIN_LAT
        for y in range(2):
            off = ((x * 2 + y) * WIN_LAT + u) * HALF_POS
            tprime[xu * 16 : xu * 16 + HEADS, y * HALF_POS : (y + 1) * HALF_POS] = table[
                :, off : off + HALF_POS
            ]
    rows = tprime[...].astype(bf16)
    for c in range(WIN_LON):
        part = nn(rows, sel_ref[c])
        for half in range(2):
            base = half * SCATTER + c * 192
            bias[base : base + 192, :] = part[:, half * 128 : half * 128 + 128]


def same_region(reg_ref, regs):
    regs[0:WIN_LAT, 0:WIN_LON] = reg_ref[0].astype(f32)
    regs[WIN_LAT:ROWS, 0:WIN_LON] = reg_ref[1].astype(f32)
    grid = regs[0:ROWS, 0:WIN_LON].astype(bf16)
    place = iota((ROWS, WIDE), 1)
    spread = nn(grid, (place // ROWS == iota((ROWS, WIDE), 0)).astype(bf16))
    row = jnp.sum(
        jnp.where(place % ROWS == iota((ROWS, WIDE), 0), spread, 0.0), axis=0, keepdims=True
    )
    kind = iota((16, WIDE), 0).astype(f32)
    hot = jnp.where((row == kind) & (iota((16, WIDE), 1) < CELLS), 1.0, 0.0)
    return tn(hot[:, :CELLS].astype(bf16), hot.astype(bf16)) > 0.5


def pad_cells(a):
    return jnp.concatenate([a, jnp.zeros((WIDE - CELLS, a.shape[1]), a.dtype)], axis=0)


def window_math(
    win, gain_ref, win_ref, wout_ref, reg_ref, sel_ref, field_ref, cot_ref, back_ref, feat_ref,
    out_back, out_sums, out_tiles_store, bias, dsf, dpt, att, tabf, regs, qkv_s,
):
    scale = HEAD_DIM ** -0.5
    cells = nn(field_ref[...], win)
    cot = nn(cot_ref[...], win)
    cot_low = cot.astype(bf16)
    centred = cells - jnp.mean(cells, axis=1, keepdims=True)
    inv_std = lax.rsqrt(jnp.mean(centred * centred, axis=1, keepdims=True) + norm_eps)
    normalized = centred * inv_std
    gain = gain_ref[...]
    normed = (normalized * gain).astype(bf16)
    qkv_s[:, : 3 * D] = nn(normed, win_ref[...]).astype(bf16)
    qkv_s[:, 3 * D :] = nt(cot_low, wout_ref[...]).astype(bf16)
    normed_t = nt(feat_ref[...], normed).astype(bf16)
    eye = (iota((128, 128), 0) == iota((128, 128), 1)).astype(bf16)
    same = same_region(reg_ref, regs)
    lane = iota((CELLS, 128), 1) // HEAD_DIM

    for g in range(3):
        lo = g * 128
        q = qkv_s[:, lo : lo + 128]
        k = pad_cells(qkv_s[:, D + lo : D + lo + 128])
        v = pad_cells(qkv_s[:, 2 * D + lo : 2 * D + lo + 128])
        do = qkv_s[:, 3 * D + lo : 3 * D + lo + 128]
        q_t = nt(eye, q).astype(bf16)
        k_t = nt(eye, k).astype(bf16)
        v_t = nt(eye, v).astype(bf16)
        do_t = nt(eye, do).astype(bf16)
        zero = jnp.zeros_like(q)
        for e in range(4):
            h = g * 4 + e
            r = e * HEAD_DIM
            mine = lane == e
            s = nt(jnp.where(mine, q, zero), k) * scale + head_rows(bias, h)
            s = jnp.where(same, s, masked_score)
            s = jnp.exp(s - jnp.max(s, axis=1, keepdims=True))
            p = s * (1.0 / jnp.sum(s, axis=1, keepdims=True))
            p_low = p.astype(bf16)
            att[h * 32 : h * 32 + 32, :] = nt(v_t[r : r + 32], p_low).astype(bf16)
            dp = nt(jnp.where(mine, do, zero), v)
            dpt[2 * D + h * 32 : 2 * D + h * 32 + 32, :] = nn(do_t[r : r + 32], p_low)[
                :, :CELLS
            ].astype(bf16)
            ds = p * (dp - jnp.sum(p * dp, axis=1, keepdims=True))
            put_head_rows(dsf, h, ds)
            ds_low = (ds * scale).astype(bf16)
            dpt[h * 32 : h * 32 + 32, :] = nt(k_t[r : r + 32], ds_low).astype(bf16)
            dpt[D + h * 32 : D + h * 32 + 32, :] = nn(q_t[r : r + 32], ds_low)[:, :CELLS].astype(
                bf16
            )
    for h in range(HEADS, 16):
        put_head_rows(dsf, h, jnp.zeros((CELLS, WIDE), f32))

    att_t = nn(feat_ref[...], att[...]).astype(bf16)
    for b in range(4):
        if b < 3:
            block = nt(normed_t, dpt[b * D : (b + 1) * D, :]).astype(bf16)
        else:
            block = nn(att_t, cot_low).astype(bf16)
        for core in range(2):
            for x in range(4):
                r = (core * 4 + x) * 48
                for t in range(3):
                    out_sums[core, x * 4 + b, t * 3 : t * 3 + 3] = block[
                        r : r + 48, t * 128 : t * 128 + 128
                    ].reshape(3, 16, 128)

    shifted_t = nn(win_ref[...], dpt[...]).astype(bf16)
    eye_c = (iota((CELLS, CELLS), 0) == iota((CELLS, CELLS), 1)).astype(bf16)
    g_normed = nt(eye_c, shifted_t)
    scaled = g_normed * gain
    grad = cot + inv_std * (
        scaled
        - jnp.mean(scaled, axis=1, keepdims=True)
        - normalized * jnp.mean(scaled * normalized, axis=1, keepdims=True)
    )
    out_back[...] = nn(back_ref[...], grad.astype(bf16)).astype(bf16).reshape(4, BACK, D)
    grad_gain = jnp.sum(g_normed * normalized, axis=0, keepdims=True)

    acc = jnp.zeros((192, 2 * HALF_POS), f32)
    for c in range(WIN_LON):
        part = jnp.concatenate(
            [dsf[pl.ds(half * SCATTER + c * 192, 192), :] for half in range(2)], axis=1
        )
        acc = acc + nt(part.astype(bf16), sel_ref[c])
    tabf[:, 25 * 128 : 32 * 128] = jnp.zeros((16, 7 * 128), f32)
    for xu in range(ROWS):
        x, u = xu // WIN_LAT, xu % WIN_LAT
        for y in range(2):
            off = ((x * 2 + y) * WIN_LAT + u) * HALF_POS
            tabf[:, off : off + HALF_POS] = acc[
                xu * 16 : xu * 16 + 16, y * HALF_POS : (y + 1) * HALF_POS
            ]
    for k in range(3):
        tabf[k : k + 1, GAIN_TILE * 128 : GAIN_TILE * 128 + 128] = grad_gain[
            :, k * 128 : k * 128 + 128
        ]
    for t in range(32):
        out_sums[t // 16, t % 16, 9] = tabf[:, t * 128 : t * 128 + 128].astype(bf16)


def local_kernel(
    win_r, gain_ref, win_ref, wout_ref, table_ref, reg_ref, sel_ref, field_ref, cot_ref, back_ref,
    feat_ref, out_back, out_sums, tprime, bias, dsf, dpt, att, tabf, regs, qkv_s,
):
    expand_table(table_ref, sel_ref, tprime, bias)
    window_math(
        win_r[...].reshape(4 * SLOT, D), gain_ref, win_ref, wout_ref, reg_ref, sel_ref, field_ref,
        cot_ref, back_ref, feat_ref, out_back, out_sums, None, bias, dsf, dpt, att, tabf, regs,
        qkv_s,
    )


LOCAL_SCRATCH = [
    VMEM((192, 2 * HALF_POS), f32),
    VMEM((2 * SCATTER, 128), f32),
    VMEM((2 * SCATTER, 128), f32),
    VMEM((3 * D, CELLS), bf16),
    VMEM((D, CELLS), bf16),
    VMEM((16, 32 * 128), f32),
    VMEM((16, 128), f32),
    VMEM((CELLS, 4 * D), bf16),
]


def local_call(win, norm_gain, input_weight, output_weight, bias_table, regions):
    field, cot, back = gather_matrices()
    consts = [jnp.asarray(a, bf16) for a in (bias_selectors(), field, cot, back, feature_order())]
    return pl.pallas_call(
        local_kernel,
        out_shape=(
            jax.ShapeDtypeStruct((4, BACK, D), bf16),
            jax.ShapeDtypeStruct((2, CHIPS, CHUNK, 16, 128), bf16),
        ),
        in_specs=[pl.BlockSpec(memory_space=VMEM)] * 11,
        out_specs=[pl.BlockSpec(memory_space=VMEM)] * 2,
        scratch_shapes=LOCAL_SCRATCH,
        compiler_params=pltpu.CompilerParams(vmem_limit_bytes=48 * 1024 * 1024),
        name="window_gradients",
    )(win, norm_gain.reshape(1, D), input_weight, output_weight, bias_table, regions, *consts)


def place():
    lon, lat = lax.axis_index("lon"), lax.axis_index("lat")
    x, z_hi, y, core = lon // 16, (lon // 8) % 2, (lon // 2) % 4, lon % 2
    return x, y, z_hi * 8 + lat, core


def at(x, y, z, core):
    return {"lon": ((x * 2 + z // 8) * 4 + y) * 2 + core, "lat": z % 8}


def window_owner(ha, ho, sign):
    lon, lat = lax.axis_index("lon"), lax.axis_index("lat")
    return {"lon": (lon + sign * ho + 64) % 64, "lat": (lat + sign * ha + 8) % 8}


def greet(partners):
    barrier = pltpu.get_barrier_semaphore()
    for partner in partners:
        pl.semaphore_signal(barrier, inc=1, device_id=partner, device_id_type=pl.DeviceIdType.MESH)
    pl.semaphore_wait(barrier, len(partners))


def remote(src, dst, send, recv, device):
    return pltpu.make_async_remote_copy(
        src_ref=src, dst_ref=dst, send_sem=send, recv_sem=recv, device_id=device,
        device_id_type=pl.DeviceIdType.MESH,
    )


QUADS = ((0, 0), (0, 1), (1, 0), (1, 1))


def halo_kernel(field_ref, cot_ref, out_ref, stage, send, land, send_sem, recv_sem):
    for quad, (ha, ho) in enumerate(QUADS):
        base = quad * SLOT
        stage[base + 2 * QUAD : base + SLOT, :] = jnp.zeros((SLOT - 2 * QUAD, D), f32)
        for which, ref in enumerate((field_ref, cot_ref)):
            for lev in range(2):
                for a in range(3):
                    row = base + which * QUAD + (lev * 3 + a) * 6
                    part = ref[1 - lev, a + 3 * (1 - ha)].astype(f32)
                    stage[row : row + 6, :] = part[6:12] if ho == 0 else part[0:6]
    send[...] = stage[...].astype(bf16).reshape(4, SLOT, D)
    greet([window_owner(ha, ho, sign) for ha, ho in QUADS[1:] for sign in (-1, 1)])
    copies = []
    for quad in (3, 1, 2):
        ha, ho = QUADS[quad]
        copies.append(
            remote(
                send.at[quad], land.at[quad], send_sem.at[quad], recv_sem.at[quad],
                window_owner(ha, ho, -1),
            )
        )
        copies[-1].start()
    out_ref[0] = send[0]
    for copy in copies:
        copy.wait_recv()
    for quad in range(1, 4):
        out_ref[quad] = land[quad]
    for copy in copies:
        copy.wait_send()


def halo_call(latent_field, cotangent):
    return pl.pallas_call(
        halo_kernel,
        out_shape=jax.ShapeDtypeStruct((4, SLOT, D), bf16),
        in_specs=[pl.BlockSpec(memory_space=VMEM)] * 2,
        out_specs=pl.BlockSpec(memory_space=VMEM),
        scratch_shapes=[
            VMEM((4 * SLOT, D), f32),
            VMEM((4, SLOT, D), bf16),
            VMEM((4, SLOT, D), bf16),
            pltpu.SemaphoreType.DMA((4,)),
            pltpu.SemaphoreType.DMA((4,)),
        ],
        compiler_params=pltpu.CompilerParams(
            collective_id=0, has_side_effects=True, vmem_limit_bytes=48 * 1024 * 1024
        ),
        name="halo",
    )(latent_field, cotangent)


def sums_kernel(
    back_ref, sums_ref, out_field, out_win, out_wout, out_gain, out_table,
    back_land, back_stage, pair, mine, chips, total, zland, owned, gathered, zhi_land, rows32, rows_send,
    rows_land, table, back_send_sem, back_recv_sem, pair_send, pair_recv, chip_send, chip_recv,
    z_send, z_recv, zg_send, zg_recv, hi_sem, tab_send, tab_recv, row_send, row_recv, last_sem,
):
    x, y, z, core = place()
    xy = x * 4 + y

    def shifted(k):
        return (x + k // 4) % 4, (y + k % 4) % 4

    def before(k):
        return (x - k // 4 + 4) % 4, (y - k % 4 + 4) % 4

    partners = [window_owner(ha, ho, sign) for ha, ho in QUADS[1:] for sign in (-1, 1)]
    partners.append(at(x, y, z, 1 - core))
    partners += [at(*shifted(k), z, core) for k in range(1, CHIPS)]
    partners += [at(x, y, (z + k) % 16, core) for k in range(1, 16)]
    greet(partners)

    order = list(range(1, CHIPS)) + [0]
    pairs = []
    for k in order:
        tx, ty = shifted(k)
        pairs.append(
            remote(
                sums_ref.at[1 - core, tx * 4 + ty], pair.at[k], pair_send.at[k], pair_recv.at[k],
                at(x, y, z, 1 - core),
            )
        )
        pairs[-1].start()
    backs = []
    for quad in (3, 1, 2):
        ha, ho = QUADS[quad]
        backs.append(
            remote(
                back_ref.at[quad], back_land.at[quad], back_send_sem.at[quad],
                back_recv_sem.at[quad], window_owner(ha, ho, 1),
            )
        )
        backs[-1].start()
    sends = []
    for k, copy in zip(order, pairs):
        copy.wait_recv()
        tx, ty = shifted(k)
        part = sums_ref[core, tx * 4 + ty].astype(f32) + pair[k].astype(f32)
        if k:
            mine[k] = part.astype(bf16)
            sends.append(
                remote(
                    mine.at[k], chips.at[k], chip_send.at[k], chip_recv.at[k], at(tx, ty, z, core)
                )
            )
            sends[-1].start()
        else:
            acc = part
    for k, copy in zip(order, sends):
        copy.wait_recv()
        acc = acc + chips[k].astype(f32)
    total[...] = acc.astype(bf16)

    gain_here = (core == GAIN_TILE // CORE_TILES) & (xy == GAIN_TILE % CORE_TILES)
    hi = remote(
        total.at[9], zhi_land, hi_sem.at[0], hi_sem.at[1], at(x, y, (z + 8) % 16, core)
    )
    hi.start()

    def to_owner(t):
        return remote(
            total.at[t], zland.at[(z - t + 16) % 16], z_send.at[t], z_recv.at[(z - t + 16) % 16],
            at(x, y, t, core),
        )

    for t in range(CHUNK):
        active = (z != t) if t < 9 else (z != t) & gain_here

        @pl.when(active)
        def _(t=t):
            to_owner(t).start()

    owner = (z < 9) | ((z == 9) & gain_here)

    def spread(k):
        return remote(
            owned, gathered.at[z], zg_send.at[k], zg_recv.at[z], at(x, y, (z + k) % 16, core)
        )

    @pl.when(owner)
    def _():
        acc = total[z].astype(f32)
        for k in range(1, 16):
            remote(total.at[0], zland.at[k], z_send.at[0], z_recv.at[k], at(x, y, z, core)).wait_recv()
            acc = acc + zland[k].astype(f32)
        owned[...] = acc.astype(bf16)
        for k in range(1, 16):
            spread(k).start()
        gathered[z] = owned[...]

    for t in range(CHUNK):
        active = (z != t) if t < 9 else (z != t) & gain_here

        @pl.when(active)
        def _(t=t):
            to_owner(t).wait_send()
            remote(
                owned, gathered.at[t], zg_send.at[0], zg_recv.at[t], at(x, y, z, core)
            ).wait_recv()

    hi.wait()
    tile = total[9].astype(f32) + zhi_land[...].astype(f32)
    summed = gathered[9].astype(f32)
    table[core * CORE_TILES + xy] = jnp.where(gain_here, summed, tile).astype(bf16)

    for t in range(9):
        rows32[(t % 3) * 16 : (t % 3) * 16 + 16, (t // 3) * 128 : (t // 3) * 128 + 128] = gathered[
            t
        ].astype(f32)
    z_hi = z // 8
    mine_z = rows32[pl.ds(pl.multiple_of(z_hi * 24, 8), 24), :]
    for to in range(4):
        part = mine_z[to * 6 : to * 6 + 6]
        rows_send[to] = jnp.concatenate([part, jnp.zeros((10, D), f32)], axis=0).astype(bf16)
    row_copies = []
    for k in range(1, 4):
        row_copies.append(
            remote(
                rows_send.at[(y + k) % 4], rows_land.at[y], row_send.at[k], row_recv.at[k],
                at(x, (y + k) % 4, z, core),
            )
        )
        row_copies[-1].start()
    slot = core * CORE_TILES + xy
    tab_copies = []
    for k in range(1, CHIPS):
        tab_copies.append(
            remote(
                table.at[slot], table.at[slot], tab_send.at[k], tab_recv.at[k],
                at(*shifted(k), z, core),
            )
        )
        tab_copies[-1].start()
    rows_land[y] = rows_send[y]
    for copy in backs:
        copy.wait_recv()
    for quad, (ha, ho) in enumerate(QUADS):
        block = (back_ref if quad == 0 else back_land)[quad].astype(f32)
        for lev in range(2):
            for a in range(3):
                row = (lev * 3 + a) * 6
                cell = ((1 - lev) * 6 + a + 3 * (1 - ha)) * 16 + 6 * (1 - ho)
                back_stage[cell : cell + 6, :] = block[row : row + 6]
    for lev in range(2):
        for a in range(6):
            cell = (lev * 6 + a) * 16
            out_field[lev, a] = back_stage[cell : cell + 16, :][:12].astype(bf16)
    for copy in tab_copies:
        copy.wait_recv()
    half = table.at[pl.ds(core * CORE_TILES, CORE_TILES)]
    last = remote(half, half, last_sem.at[0], last_sem.at[1], at(x, y, z, 1 - core))
    last.start()
    factor = 1.0 / math.sqrt(512 * CELLS)
    for copy in row_copies:
        copy.wait_recv()
    for b in range(4):
        rows = (rows_land[b].astype(f32) * factor)[:6].astype(bf16)
        if b < 3:
            out_win[:, b * D : (b + 1) * D] = rows
        else:
            out_wout[...] = rows
    last.wait_recv()
    for t in range(26):
        width = min(128, POS - t * 128)
        out_table[0, :, t * 128 : t * 128 + width] = table[t].astype(f32)[:HEADS, :width]
    gains = table[GAIN_TILE].astype(f32) * factor
    for k in range(3):
        out_gain[:, k * 128 : k * 128 + 128] = gains[k : k + 1]
    for copy in pairs + backs + sends + row_copies + tab_copies + [last]:
        copy.wait_send()

    @pl.when(owner)
    def _():
        for k in range(1, 16):
            spread(k).wait_send()


def sums_call(back, sums):
    tile = (16, 128)
    sem = pltpu.SemaphoreType.DMA
    return pl.pallas_call(
        sums_kernel,
        out_shape=(
            jax.ShapeDtypeStruct((LEV, WIN_LAT, WIN_LON, D), bf16),
            jax.ShapeDtypeStruct((6, 3 * D), bf16),
            jax.ShapeDtypeStruct((6, D), bf16),
            jax.ShapeDtypeStruct((1, D), f32),
            jax.ShapeDtypeStruct((1, HEADS, POS), f32),
        ),
        in_specs=[pl.BlockSpec(memory_space=VMEM)] * 2,
        out_specs=[pl.BlockSpec(memory_space=VMEM)] * 5,
        scratch_shapes=[
            VMEM((4, BACK, D), bf16),
            VMEM((ROWS * 16, D), f32),
            VMEM((CHIPS, CHUNK) + tile, bf16),
            VMEM((CHIPS, CHUNK) + tile, bf16),
            VMEM((CHIPS, CHUNK) + tile, bf16),
            VMEM((CHUNK,) + tile, bf16),
            VMEM((16,) + tile, bf16),
            VMEM(tile, bf16),
            VMEM((16,) + tile, bf16),
            VMEM(tile, bf16),
            VMEM((48, D), f32),
            VMEM((4, 16, D), bf16),
            VMEM((4, 16, D), bf16),
            VMEM((32,) + tile, bf16),
            sem((4,)), sem((4,)), sem((CHIPS,)), sem((CHIPS,)), sem((CHIPS,)), sem((CHIPS,)),
            sem((CHUNK,)), sem((16,)), sem((16,)), sem((16,)), sem((2,)), sem((CHIPS,)),
            sem((CHIPS,)), sem((4,)), sem((4,)), sem((2,)),
        ],
        compiler_params=pltpu.CompilerParams(
            collective_id=1, has_side_effects=True, vmem_limit_bytes=48 * 1024 * 1024
        ),
        name="sums",
    )(back, sums)


def on_device(latent_field, cotangent, norm_gain, input_weight, output_weight, bias_table, regions):
    win = halo_call(latent_field, cotangent)
    back, sums = local_call(win, norm_gain, input_weight, output_weight, bias_table, regions)
    field, grad_in, grad_out, gain, table = sums_call(back, sums)
    return field, grad_in, grad_out, gain.reshape(D), table


def solution(mesh):
    in_specs = (
        P(None, "lat", "lon", None),
        P(None, "lat", "lon", None),
        P(),
        P(),
        P(),
        P("lat", None, None),
        P(None, "lat", "lon"),
    )
    out_specs = (
        P(None, "lat", "lon", None),
        P("lon", None),
        P("lon", None),
        P(),
        P("lat", None, None),
    )
    return jax.shard_map(
        on_device, mesh=mesh, in_specs=in_specs, out_specs=out_specs, check_vma=False
    )
```

time: 1260 us -> 105 us (0.08)
  blocking collectives: 610 us -> 0 us
  waiting for transfers between devices: 490 us -> 0 us
  Pallas kernels: 0 us -> 89.4 us
  local copies, waits for them, and re-layouts: 71.6 us -> 14.1 us
  matrix products: 37.8 us -> 0 us
  starting transfers between devices: 23.4 us -> 0 us
  other arithmetic: 15.2 us -> 0.6 us
  between operations: 15.1 us -> 0.68 us
    unnamed x1 -> x0, blocking collectives: 583 us -> none
    psum x2 -> x0, waiting for transfers between devices: 490 us -> none  [the longest x1 408 us: on_device(): grad_gain, grad_table = lax.psum((grad_gain, grad_table), 'lon')]
    pallas_call x0 -> x3, Pallas kernels: none -> 89.4 us  [the longest x1 60.9 us: sums_call(): pl.pallas_call(sums_kernel, out_shape=(jax.ShapeDtypeStruct((LEV, WIN_LAT...]
    dot_general x13 -> x0, matrix products: 37.8 us -> none  [the longest x1 13 us: fold_bias(): jnp.einsum('bhxucyvd,cdr->bhxyuvr', shaped, longitude_onehot(WIN_LON), pr...]
    another operation x4 -> x0, local copies, waits for them, and re-layouts: 31.7 us -> none
    reshape x2 -> x1, local copies, waits for them, and re-layouts: 31.9 us -> 0.68 us  [local_call(): norm_gain.reshape(1, D)]
    psum x1 -> x0, blocking collectives: 26.6 us -> none  [on_device(): lax.psum(grad_gain.astype(jnp.bfloat16), 'lat').astype(jnp.float32)]
    ppermute x4 -> x0, starting transfers between devices: 23.2 us -> none  [from_behind(): return lax.ppermute(value, axis, pairs)]
  transfers between devices with their start and end apart: 6 -> 0, of which waited for: 2 -> 0; matrix products, arithmetic and copies ran while one was open for 8% -> 0% of each run, Pallas kernels for 0% -> 0%
where the time goes in v1:
time: 105 us
  Pallas kernels  89.4 us (85%)
  local copies, waits for them, and re-layouts  14.1 us (13%)
    pallas_call x1, Pallas kernels, sums_call(): pl.pallas_call(sums_kernel, out_shape=(jax.ShapeDtypeStruct((LEV, WIN_LAT...  60.9 us
    pallas_call x1, Pallas kernels, halo_call(): pl.pallas_call(halo_kernel, out_shape=jax.ShapeDtypeStruct((4, SLOT, D),...  16.7 us
    unnamed x23, local copies, waits for them, and re-layouts  13.4 us
    pallas_call x1, Pallas kernels, local_call(): pl.pallas_call(local_kernel, out_shape=(jax.ShapeDtypeStruct((4, BACK, D)...  11.8 us

profile of v1, /device:TPU:1, one launch (start us, length us, event | category | flops | bytes accessed | tf_op | source)
XLA Modules:
  0.0 104.8 jit_solution(13260823709791333096)
XLA Ops:
  0.6 0.7 reshape.16.gain_ref
  1.3 0.7 copy.19.reg_ref
  2.0 0.9 copy.17.field_ref
  2.9 0.9 copy.18.cot_ref
  3.8 16.7 %halo.1.win_r = bf16[4,80,384]{2,1,0:T(8,128)(2,1)S(1)} custom-call(bf16[2,6,12,384]{3,2,1,0:T(8,128)(2,1)S(1)} %copy.17.field_ref, bf16[2,6,12,384]{3,2,1,0:T(8,128)(2,1)S(1)} %copy.18.cot_ref), custom_call_target="tpu_custom_call" | custom-call | tf_op jit(solution)/shard_map/halo/pallas_call | solution.py:352
  20.6 0.0 copy-start
  20.6 1.5 %copy-done = bf16[12,276,256]{2,1,0:T(8,128)(2,1)S(1)} copy-done((bf16[12,276,256]{2,1,0:T(8,128)(2,1)S(1)}, bf16[12,276,256]{2,1,0:T(8,128)(2,1)}, u32[]{:S(2)}) %copy-start) | copy-done | bytes 1695768
  22.1 0.0 copy-start.1
  22.1 1.2 %copy-done.1 = bf16[384,1152]{1,0:T(8,128)(2,1)S(1)} copy-done((bf16[384,1152]{1,0:T(8,128)(2,1)S(1)}, bf16[384,1152]{1,0:T(8,128)(2,1)}, u32[]{:S(2)}) %copy-start.1) | copy-done | bytes 884760
  23.2 0.0 copy-start.2
  23.2 1.0 copy-done.2
  24.2 0.0 copy-start.3
  24.2 1.0 copy-done.3
  25.1 0.9 copy-done.4
  26.0 0.9 copy-done.5
  26.9 0.9 copy-done.6
  27.8 0.9 copy-done.7
  28.7 11.8 %window_gradients.1 = (bf16[4,48,384]{2,1,0:T(8,128)(2,1)S(1)}, bf16[2,16,10,16,128]{4,3,2,1,0:T(8,128)(2,1)S(1)}) custom-call(bf16[4,80,384]{2,1,0:T(8,128)(2,1)S(1)} %halo.1.win_r, f32[1,384]{1,0:T(1,128)S(1)} %reshape.16.gain_ref, bf16[384,1152]{1,0:T(8,128)(2,1)S(1)} %copy-done.1, bf16[384,384]{1,0:T(8,128)(2,1)S(1)} %copy-done.2, ...), custom_call_target="tpu_custom_call" | custom-call | tf_op jit(solution)/shard_map/window_gradients/pallas_call | solution.py:274
  40.5 60.9 %sums.1 = (bf16[2,6,12,384]{3,2,1,0:T(8,128)(2,1)S(1)}, bf16[6,1152]{1,0:T(8,128)(2,1)S(1)}, bf16[6,384]{1,0:T(8,128)(2,1)S(1)}, f32[1,384]{1,0:T(1,128)S(1)}, f32[1,12,3312]{2,1,0:T(8,128)S(1)}) custom-call(bf16[4,48,384]{2,1,0:T(8,128)(2,1)S(1)} %get-tuple-element.12.back_ref, bf16[2,16,10,16,128]{4,3,2,1,0:T(8,128)(2,1)S(1)} %get-tuple-element.13.sums_ref), custom_call_target="tpu_custom_call" | custom-call | tf_op jit(solution)/shard_map/sums/pallas_call | solution.py:560
  101.4 0.7 copy.20
  102.1 0.6 reduce
  102.7 0.8 copy.21
  103.6 0.6 copy.24
  104.2 0.6 copy.25
  (4 shorter events, 0.0 us)
Async XLA Ops:
  20.6 1.5 %copy-start = (bf16[12,276,256]{2,1,0:T(8,128)(2,1)S(1)}, bf16[12,276,256]{2,1,0:T(8,128)(2,1)}, u32[]{:S(2)}) copy-start(bf16[12,276,256]{2,1,0:T(8,128)(2,1)} %constant.10.clone.sel_ref) | copy-start | bytes 5087236
  22.1 1.2 %copy-start.1 = (bf16[384,1152]{1,0:T(8,128)(2,1)S(1)}, bf16[384,1152]{1,0:T(8,128)(2,1)}, u32[]{:S(2)}) copy-start(bf16[384,1152]{1,0:T(8,128)(2,1)} %win_ref.1) | copy-start | bytes 2654212
  23.2 1.0 copy-start.2
  24.2 1.0 copy-start.3
  25.1 0.9 copy-start.4
  26.0 0.9 copy-start.5
  26.9 0.9 copy-start.6
  27.8 0.9 copy-start.7

commit v2 on v0

v2 whole, which is shorter than its diff:
```python
import functools
import math

import jax
import jax.numpy as jnp
import numpy as np
from jax import lax
from jax.experimental import pallas as pl
from jax.experimental.pallas import tpu as pltpu
from jax.sharding import PartitionSpec as P

D = 384
HEADS = 12
HEAD_DIM = 32
LEV = 2
WIN_LAT = 6
WIN_LON = 12
CELLS = 144
ROWS = LEV * WIN_LAT
SPREAD = 2 * WIN_LON - 1
HALF_POS = WIN_LAT * SPREAD
POS = 3312
WIDE = 256
CHIPS = 16
TOKENS = 512 * CELLS
TABLE_TILES = 26
GROUPS = 3
KEEP = 80
SCATTER = WIN_LON * ROWS * 16

norm_eps = 1e-05
masked_score = -1000000000.0
VMEM = pltpu.VMEM
f32 = jnp.float32
bf16 = jnp.bfloat16


def feature_order():
    out = np.zeros((2, 512, D), np.float32)
    for core in range(2):
        for x in range(4):
            for y in range(4):
                for z_hi in range(2):
                    lon = ((x * 2 + z_hi) * 4 + y) * 2 + core
                    for k in range(6):
                        row = ((core * 4 + x) * 4 + y) * 16 + z_hi * 6 + k
                        out[0, row, lon * 6 + k] = 1
                        out[1, row + 4, lon * 6 + k] = 1
    return out


def bias_selectors():
    out = np.zeros((WIN_LON, 2 * HALF_POS, WIDE), np.float32)
    for c in range(WIN_LON):
        for p in range(CELLS):
            d, v, lev = p // ROWS, (p % ROWS) // 2, 1 - p % 2
            out[c, lev * HALF_POS + v * SPREAD + c - d + WIN_LON - 1, p] = 1
    return out


def table_offset(row, y):
    x, u = 1 - row % 2, row // 2
    return ((x * 2 + y) * WIN_LAT + u) * HALF_POS


def head_rows(ref, h):
    return jnp.concatenate(
        [ref[pl.ds(half * SCATTER + h, CELLS, stride=16), :] for half in range(2)], axis=1
    )


def put_head_rows(ref, h, value):
    for half in range(2):
        ref[pl.ds(half * SCATTER + h, CELLS, stride=16), :] = value[:, half * 128 : half * 128 + 128]


def nt(a, b):
    return lax.dot_general(a, b, (((1,), (1,)), ((), ())), preferred_element_type=f32)


def nn(a, b):
    return lax.dot_general(a, b, (((1,), (0,)), ((), ())), preferred_element_type=f32)


def tn(a, b):
    return lax.dot_general(a, b, (((0,), (0,)), ((), ())), preferred_element_type=f32)


def iota(shape, dim):
    return lax.broadcasted_iota(jnp.int32, shape, dim)


def place():
    lon, lat = lax.axis_index("lon"), lax.axis_index("lat")
    x, z_hi, y, core = lon // 16, (lon // 8) % 2, (lon // 2) % 4, lon % 2
    return x, y, z_hi * 8 + lat, core


def at(x, y, z, core):
    return {"lon": ((x * 2 + z // 8) * 4 + y) * 2 + core, "lat": z % 8}


def window_owner(ha, ho, sign):
    lon, lat = lax.axis_index("lon"), lax.axis_index("lat")
    return {"lon": (lon + sign * ho + 64) % 64, "lat": (lat + sign * ha + 8) % 8}


def greet(partners):
    barrier = pltpu.get_barrier_semaphore()
    for partner in partners:
        pl.semaphore_signal(barrier, inc=1, device_id=partner, device_id_type=pl.DeviceIdType.MESH)
    return len(partners)


def greeted(count):
    pl.semaphore_wait(pltpu.get_barrier_semaphore(), count)


def remote(src, dst, send, recv, device):
    return pltpu.make_async_remote_copy(
        src_ref=src, dst_ref=dst, send_sem=send, recv_sem=recv, device_id=device,
        device_id_type=pl.DeviceIdType.MESH,
    )


QUADS = ((0, 0), (0, 1), (1, 0), (1, 1))


def cells_part(ref, ha, ho):
    return ref.at[pl.ds(3 * (1 - ha), 3), pl.ds(6 * (1 - ho), 6)]


def window_part(ref, ha, ho):
    return ref.at[pl.ds(3 * ha, 3), pl.ds(6 * ho, 6)]


def halo_partners():
    return [window_owner(ha, ho, sign) for ha, ho in QUADS[1:] for sign in (-1, 1)]


def expand_table(table, sel_ref, tprime, bias):
    table = table[0].astype(f32)
    tprime[...] = jnp.zeros_like(tprime)
    for row in range(ROWS):
        for y in range(2):
            off = table_offset(row, y)
            tprime[row * 16 : row * 16 + HEADS, y * HALF_POS : (y + 1) * HALF_POS] = table[
                :, off : off + HALF_POS
            ]
    rows = tprime[...].astype(bf16)
    for c in range(WIN_LON):
        part = nn(rows, sel_ref[c])
        for half in range(2):
            base = half * SCATTER + c * 192
            bias[base : base + 192, :] = part[:, half * 128 : half * 128 + 128]


def same_region(reg, regs):
    for a in range(WIN_LAT):
        for lev in range(2):
            regs[a * 2 + lev : a * 2 + lev + 1, 0:WIN_LON] = reg[a, 1 - lev : 2 - lev].astype(f32)
    grid = regs[0:ROWS, 0:WIN_LON].astype(bf16)
    where = iota((ROWS, WIDE), 1)
    spread = nn(grid, (where // ROWS == iota((ROWS, WIDE), 0)).astype(bf16))
    row = jnp.sum(
        jnp.where(where % ROWS == iota((ROWS, WIDE), 0), spread, 0.0), axis=0, keepdims=True
    )
    kind = iota((16, WIDE), 0).astype(f32)
    hot = jnp.where((row == kind) & (iota((16, WIDE), 1) < CELLS), 1.0, 0.0)
    return tn(hot[:, :CELLS].astype(bf16), hot.astype(bf16))


def cells_to_rows(land, stage):
    for a in range(WIN_LAT):
        for o in range(WIN_LON):
            p = o * ROWS + a * 2
            stage[p : p + 2, :] = land[a, o].astype(f32)


def pad_cells(a):
    return jnp.concatenate([a, jnp.zeros((WIDE - CELLS, a.shape[1]), a.dtype)], axis=0)


def keep_rows():
    shape = (2 * KEEP, CELLS + 16)
    row, col = iota(shape, 0), iota(shape, 1)
    half, w = row // KEEP, row % KEEP
    own = (w // 6) * 12 + half * 6 + w % 6
    gain = CELLS + HEADS + jnp.minimum(w - 72, 3)
    return (col == jnp.where(w < 72, own, gain)).astype(bf16)


FAR_FIRST = (10, 6, 9, 11, 14, 2, 8, 5, 7, 13, 15, 1, 3, 4, 12)


def window_kernel(
    field_hbm, cot_hbm, gain_hbm, win_hbm, wout_hbm, table_hbm, reg_hbm, sel_hbm, feat_hbm,
    field_out, rows_out, table_out,
    field_land, cot_land, gain_v, w_in, w_out, table, reg, sel, feat, tprime, regs, stage,
    qkv, normt, bias, probs, dsf, dpt, att, tabf, grad_rows, gwin,
    sums, pair, mine, chips, tsums, tpair, tmine, tchips, plane_sums, pack, pack_land, owned, zland,
    hi_land,
    load_sem, own_sem, halo_send, halo_recv, back_send, back_recv, core_send, core_recv, chip_send,
    chip_recv, z_send, z_recv, zp_sem, hi_sem, tab_send, tab_recv, last_sem,
):
    x, y, z, core = place()
    xy = x * 4 + y
    z_hi, parity = z // 8, z % 2
    z_pair = z + 1 - 2 * parity
    other_core = at(x, y, z, 1 - core)

    def plane(k):
        tx, ty = (x + k // 4) % 4, (y + k % 4) % 4
        return tx * 4 + ty, at(tx, ty, z, core)

    partners = halo_partners() + [other_core]
    partners += [plane(k)[1] for k in range(1, CHIPS)]
    partners += [at(x, y, (z + k) % 16, core) for k in range(1, 16)]
    count = greet(partners)
    owns = [
        pltpu.make_async_copy(cells_part(src, 0, 0), window_part(dst, 0, 0), own_sem.at[i])
        for i, (src, dst) in enumerate(((field_hbm, field_land), (cot_hbm, cot_land)))
    ]
    loads = [
        pltpu.make_async_copy(src, dst, load_sem.at[i])
        for i, (src, dst) in enumerate(
            (
                (table_hbm, table), (sel_hbm, sel), (reg_hbm, reg), (gain_hbm, gain_v),
                (win_hbm, w_in), (feat_hbm, feat), (wout_hbm, w_out),
            )
        )
    ]
    for copy in loads + owns:
        copy.start()
    greeted(count)

    halos = [[], []]
    for i, (src, dst) in enumerate(((field_hbm, field_land), (cot_hbm, cot_land))):
        for quad in (3, 1, 2):
            ha, ho = QUADS[quad]
            halos[i].append(
                remote(
                    cells_part(src, ha, ho), window_part(dst, ha, ho), halo_send.at[i, quad],
                    halo_recv.at[i, quad], window_owner(ha, ho, -1),
                )
            )
            halos[i][-1].start()
    for copy in loads:
        copy.wait()
    same = same_region(reg, regs) > 0.5
    expand_table(table, sel, tprime, bias)

    owns[0].wait()
    for copy in halos[0]:
        copy.wait_recv()
    cells_to_rows(field_land, stage)
    cells = stage[...]
    centred = cells - jnp.mean(cells, axis=1, keepdims=True)
    inv_std = lax.rsqrt(jnp.mean(centred * centred, axis=1, keepdims=True) + norm_eps)
    normalized = centred * inv_std
    stage[...] = normalized
    gain = gain_v[...].reshape(1, D)
    normed = (normalized * gain).astype(bf16)
    qkv[:, : 3 * D] = nn(normed, w_in[...]).astype(bf16)
    for i in range(2):
        normt[i] = nt(feat[i], normed).astype(bf16)

    scale = HEAD_DIM ** -0.5
    eye = (iota((128, 128), 0) == iota((128, 128), 1)).astype(bf16)
    lane = iota((CELLS, 128), 1) // HEAD_DIM
    zero = jnp.zeros((CELLS, 128), bf16)

    def part(which, g):
        lo = which * D + g * 128
        return qkv[:, lo : lo + 128]

    def four_heads(a):
        return jnp.concatenate([jnp.where(lane == e, a, zero) for e in range(4)], axis=0)

    for g in range(GROUPS):
        q, k, v = part(0, g), pad_cells(part(1, g)), pad_cells(part(2, g))
        v_t = nt(eye, v).astype(bf16)
        scores = nt(four_heads(q), k)
        for e in range(4):
            h = g * 4 + e
            r = e * HEAD_DIM
            s = scores[e * CELLS : (e + 1) * CELLS] * scale + head_rows(bias, h)
            s = jnp.where(same, s, masked_score)
            s = jnp.exp(s - jnp.max(s, axis=1, keepdims=True))
            p = s * (1.0 / jnp.sum(s, axis=1, keepdims=True))
            probs[h] = p
            att[h * 32 : h * 32 + 32, :] = nt(v_t[r : r + 32], p.astype(bf16)).astype(bf16)
    att_t = nn(feat[1], att[...]).astype(bf16)

    owns[1].wait()
    for copy in halos[1]:
        copy.wait_recv()
    cells_to_rows(cot_land, grad_rows)
    cot = grad_rows[...].astype(bf16)
    qkv[:, 3 * D :] = nt(cot, w_out[...]).astype(bf16)

    core_copies = [
        remote(sums.at[g, 1 - core], pair.at[g], core_send.at[g], core_recv.at[g], other_core)
        for g in range(GROUPS)
    ]
    core_copies.append(
        remote(tsums.at[1 - core], tpair, core_send.at[3], core_recv.at[3], other_core)
    )
    sends = [[], [], [], []]

    def to_plane(g):
        core_copies[g].wait_recv()
        if g < GROUPS:
            mine[g] = (sums[g, core].astype(f32) + pair[g].astype(f32)).astype(bf16)
        else:
            tmine[...] = (tsums[core].astype(f32) + tpair[...].astype(f32)).astype(bf16)
        for k in FAR_FIRST:
            index, device = plane(k)
            src, dst = (
                (mine.at[g, index], chips.at[g, k])
                if g < GROUPS
                else (tmine.at[index], tchips.at[k])
            )
            sends[g].append(remote(src, dst, chip_send.at[g, k], chip_recv.at[g, k], device))
            sends[g][-1].start()

    for g in range(GROUPS):
        q, k, v, do = part(0, g), pad_cells(part(1, g)), pad_cells(part(2, g)), part(3, g)
        q_t = nt(eye, q).astype(bf16)
        k_t = nt(eye, k).astype(bf16)
        do_t = nt(eye, do).astype(bf16)
        grad_probs = nt(four_heads(do), v)
        for e in range(4):
            h = g * 4 + e
            r = e * HEAD_DIM
            p = probs[h]
            dp = grad_probs[e * CELLS : (e + 1) * CELLS]
            dpt[2 * D + h * 32 : 2 * D + h * 32 + 32, :] = nn(do_t[r : r + 32], p.astype(bf16))[
                :, :CELLS
            ].astype(bf16)
            ds = p * (dp - jnp.sum(p * dp, axis=1, keepdims=True))
            put_head_rows(dsf, h, ds)
            ds_low = (ds * scale).astype(bf16)
            dpt[h * 32 : h * 32 + 32, :] = nt(k_t[r : r + 32], ds_low).astype(bf16)
            dpt[D + h * 32 : D + h * 32 + 32, :] = nn(q_t[r : r + 32], ds_low)[:, :CELLS].astype(
                bf16
            )
        blocks = [
            nt(normt[which % 2], dpt[which * D + g * 128 : which * D + g * 128 + 128, :])
            for which in range(3)
        ]
        blocks.append(nn(att_t, cot[:, g * 128 : g * 128 + 128]))
        b0, b1, b2, b3 = (b.reshape(32, 2, 8, 128) for b in blocks)
        sums[g] = (
            jnp.concatenate(
                [b0[:, 0], b0[:, 1] + b1[:, 0], b1[:, 1], b2[:, 0], b2[:, 1] + b3[:, 0], b3[:, 1]],
                axis=1,
            )
            .astype(bf16)
            .reshape(2, CHIPS, 48, 128)
        )
        core_copies[g].start()
        if g:
            to_plane(g - 1)

    shifted_t = nn(w_in[...], dpt[...]).astype(bf16)
    eye_c = (iota((CELLS, CELLS), 0) == iota((CELLS, CELLS), 1)).astype(bf16)
    g_normed = nt(eye_c, shifted_t)
    normalized = stage[...]
    scaled = g_normed * gain
    grad_gain = jnp.sum(g_normed * normalized, axis=0, keepdims=True)
    grad_rows[...] = cot.astype(f32) + inv_std * (
        scaled
        - jnp.mean(scaled, axis=1, keepdims=True)
        - normalized * jnp.mean(scaled * normalized, axis=1, keepdims=True)
    )
    for a in range(WIN_LAT):
        for o in range(WIN_LON):
            p = o * ROWS + a * 2
            gwin[a, o] = grad_rows[p : p + 2, :].astype(bf16)
    backs = []
    for quad in (3, 1, 2):
        ha, ho = QUADS[quad]
        backs.append(
            remote(
                window_part(gwin, ha, ho), cells_part(field_out, ha, ho), back_send.at[quad],
                back_recv.at[quad], window_owner(ha, ho, 1),
            )
        )
        backs[-1].start()
    to_plane(2)

    for h in range(HEADS, 16):
        put_head_rows(dsf, h, jnp.zeros((CELLS, WIDE), f32))
    acc = jnp.zeros((192, 2 * HALF_POS), f32)
    for c in range(WIN_LON):
        rows = jnp.concatenate(
            [dsf[pl.ds(half * SCATTER + c * 192, 192), :] for half in range(2)], axis=1
        )
        acc = acc + nt(rows.astype(bf16), sel[c])
    tabf[:, 25 * 128 : 32 * 128] = jnp.zeros((16, 7 * 128), f32)
    for row in range(ROWS):
        for half in range(2):
            off = table_offset(row, half)
            tabf[:, off : off + HALF_POS] = acc[
                row * 16 : row * 16 + 16, half * HALF_POS : (half + 1) * HALF_POS
            ]
    spare = jnp.concatenate(
        [grad_gain[:, k * 128 : k * 128 + 128] for k in range(3)] + [jnp.zeros((1, 128), f32)],
        axis=0,
    )
    for t in range(32):
        tsums[t // 16, t % 16] = jnp.concatenate(
            [tabf[0:HEADS, t * 128 : t * 128 + 128], spare], axis=0
        ).astype(bf16)
    core_copies[3].start()
    for a in range(3):
        for o in range(6):
            field_out[3 + a, 6 + o] = gwin[a, o]
    to_plane(3)

    for g in range(GROUPS):
        for copy in sends[g]:
            copy.wait_recv()
        acc = mine[g, xy].astype(f32)
        for k in range(1, CHIPS):
            acc = acc + chips[g, k].astype(f32)
        plane_sums[g * 48 : (g + 1) * 48, :] = acc.astype(bf16)
    for copy in sends[3]:
        copy.wait_recv()
    acc = tmine[xy].astype(f32)
    for k in range(1, CHIPS):
        acc = acc + tchips[k].astype(f32)
    plane_sums[CELLS : CELLS + 16, :] = acc.astype(bf16)

    pack[...] = nn(keep_rows(), plane_sums[...]).astype(bf16).reshape(2, KEEP, 128)
    swap = remote(
        pack.at[1 - parity], pack_land, zp_sem.at[0], zp_sem.at[1], at(x, y, z_pair, core)
    )
    swap.start()
    table_part = plane_sums.at[pl.ds(CELLS, 16)]
    hi = remote(table_part, hi_land, hi_sem.at[0], hi_sem.at[1], at(x, y, (z + 8) % 16, core))
    hi.start()
    swap.wait_recv()
    owned[...] = (pack[parity].astype(f32) + pack_land[...].astype(f32)).astype(bf16)

    def keeper(j):
        return parity * 8 + (z + 4 + j) % 8

    def to_keeper(j):
        return remote(
            owned, zland.at[z // 2], z_send.at[j], z_recv.at[z // 2], at(x, y, keeper(j), core)
        )

    for j in range(8):

        @pl.when(keeper(j) != z)
        def _(j=j):
            to_keeper(j).start()

    @pl.when(parity == z_hi)
    def _():
        zland[z // 2] = owned[...]

    hi.wait_recv()
    slot = core * CHIPS + xy
    table_out[slot] = (plane_sums[CELLS : CELLS + 16].astype(f32) + hi_land[...].astype(f32)).astype(
        bf16
    )
    tab_copies = []
    for k in FAR_FIRST:
        tab_copies.append(
            remote(
                table_out.at[slot], table_out.at[slot], tab_send.at[k], tab_recv.at[k], plane(k)[1]
            )
        )
        tab_copies[-1].start()

    for i in range(8):

        @pl.when(2 * i + z_hi != z)
        def _(i=i):
            remote(
                owned, zland.at[i], z_send.at[0], z_recv.at[i], at(x, y, z_pair, core)
            ).wait_recv()

    total = zland[0].astype(f32)
    for i in range(1, 8):
        total = total + zland[i].astype(f32)
    rows_out[...] = total

    for copy in tab_copies:
        copy.wait_recv()
    half = table_out.at[pl.ds(core * CHIPS, CHIPS)]
    last = remote(half, half, last_sem.at[0], last_sem.at[1], other_core)
    last.start()
    for copy in backs + [last]:
        copy.wait_recv()
    for copy in halos[0] + halos[1] + core_copies + sum(sends, []) + backs + [swap, hi, last]:
        copy.wait_send()
    for copy in tab_copies:
        copy.wait_send()
    for j in range(8):

        @pl.when(keeper(j) != z)
        def _(j=j):
            to_keeper(j).wait_send()


def window_call(*args):
    tile = (16, 128)
    grid = (WIN_LAT, WIN_LON, LEV, D)
    sem = pltpu.SemaphoreType.DMA
    return pl.pallas_call(
        window_kernel,
        out_shape=(
            jax.ShapeDtypeStruct(grid, bf16),
            jax.ShapeDtypeStruct((KEEP, 128), f32),
            jax.ShapeDtypeStruct((32,) + tile, bf16),
        ),
        in_specs=[pl.BlockSpec(memory_space=pl.ANY)] * 9,
        out_specs=[pl.BlockSpec(memory_space=VMEM)] * 3,
        scratch_shapes=[
            VMEM(grid, bf16),
            VMEM(grid, bf16),
            VMEM((D,), f32),
            VMEM((D, 3 * D), bf16),
            VMEM((D, D), bf16),
            VMEM((1, HEADS, POS), bf16),
            VMEM((WIN_LAT, LEV, WIN_LON), jnp.int32),
            VMEM((WIN_LON, 2 * HALF_POS, WIDE), bf16),
            VMEM((2, 512, D), bf16),
            VMEM((192, 2 * HALF_POS), f32),
            VMEM((16, 128), f32),
            VMEM((CELLS, D), f32),
            VMEM((CELLS, 4 * D), bf16),
            VMEM((2, 512, CELLS), bf16),
            VMEM((2 * SCATTER, 128), f32),
            VMEM((HEADS, CELLS, WIDE), f32),
            VMEM((2 * SCATTER, 128), f32),
            VMEM((3 * D, CELLS), bf16),
            VMEM((D, CELLS), bf16),
            VMEM((16, 32 * 128), f32),
            VMEM((CELLS, D), f32),
            VMEM(grid, bf16),
            VMEM((GROUPS, 2, CHIPS, 48, 128), bf16),
            VMEM((GROUPS, CHIPS, 48, 128), bf16),
            VMEM((GROUPS, CHIPS, 48, 128), bf16),
            VMEM((GROUPS, CHIPS, 48, 128), bf16),
            VMEM((2, CHIPS) + tile, bf16),
            VMEM((CHIPS,) + tile, bf16),
            VMEM((CHIPS,) + tile, bf16),
            VMEM((CHIPS,) + tile, bf16),
            VMEM((CELLS + 16, 128), bf16),
            VMEM((2, KEEP, 128), bf16),
            VMEM((KEEP, 128), bf16),
            VMEM((KEEP, 128), bf16),
            VMEM((8, KEEP, 128), bf16),
            VMEM(tile, bf16),
            sem((7,)), sem((2,)), sem((2, 4)), sem((2, 4)), sem((4,)), sem((4,)), sem((4,)),
            sem((4,)), sem((4, CHIPS)), sem((4, CHIPS)), sem((8,)), sem((8,)), sem((2,)),
            sem((2,)), sem((CHIPS,)), sem((CHIPS,)), sem((2,)),
        ],
        compiler_params=pltpu.CompilerParams(
            collective_id=0, has_side_effects=True, vmem_limit_bytes=60 * 1024 * 1024
        ),
        name="window_gradients",
    )(*args)


def finish_kernel(field, rows, table, out_field, out_win, out_wout, out_gain, out_table):
    factor = 1.0 / math.sqrt(TOKENS)
    out_field[...] = field[...]
    sums = rows[...] * factor
    for g in range(GROUPS):
        for which in range(4):
            at_row = (g * 4 + which) * 6
            part = sums[at_row : at_row + 6].astype(bf16)
            if which < 3:
                lo = which * D + g * 128
                out_win[:, lo : lo + 128] = part
            else:
                out_wout[:, g * 128 : g * 128 + 128] = part
    for k in range(3):
        out_gain[k * 128 : k * 128 + 128] = sums[72 + k]
    for t in range(TABLE_TILES):
        width = min(128, POS - t * 128)
        values = table[t].astype(f32)
        for h in range(HEADS):
            out_table[h, :, t * 128 : t * 128 + width] = values[h : h + 1, :width]


def finish_call(field, rows, table):
    return pl.pallas_call(
        finish_kernel,
        out_shape=(
            jax.ShapeDtypeStruct((WIN_LAT, WIN_LON, LEV, D), bf16),
            jax.ShapeDtypeStruct((6, 3 * D), bf16),
            jax.ShapeDtypeStruct((6, D), bf16),
            jax.ShapeDtypeStruct((D,), f32),
            jax.ShapeDtypeStruct((HEADS, 1, POS), f32),
        ),
        in_specs=[pl.BlockSpec(memory_space=VMEM)] * 3,
        out_specs=[pl.BlockSpec(memory_space=VMEM)] * 5,
        compiler_params=pltpu.CompilerParams(vmem_limit_bytes=60 * 1024 * 1024),
        name="outputs",
    )(field, rows, table)


def on_device(latent_field, cotangent, norm_gain, input_weight, output_weight, bias_table, regions):
    sel = jnp.asarray(bias_selectors(), bf16)
    feat = jnp.asarray(feature_order(), bf16)
    field, cot = (jnp.transpose(a, (1, 2, 0, 3)) for a in (latent_field, cotangent))
    reg = jnp.transpose(regions, (1, 0, 2))
    sums = window_call(
        field, cot, norm_gain, input_weight, output_weight, bias_table, reg, sel, feat
    )
    grad_field, grad_in, grad_out, grad_gain, table = finish_call(*sums)
    return (
        jnp.transpose(grad_field, (2, 0, 1, 3)),
        grad_in,
        grad_out,
        grad_gain,
        jnp.transpose(table, (1, 0, 2)),
    )


def solution(mesh):
    in_specs = (
        P(None, "lat", "lon", None),
        P(None, "lat", "lon", None),
        P(),
        P(),
        P(),
        P("lat", None, None),
        P(None, "lat", "lon"),
    )
    out_specs = (
        P(None, "lat", "lon", None),
        P("lon", None),
        P("lon", None),
        P(),
        P("lat", None, None),
    )
    return jax.shard_map(
        on_device, mesh=mesh, in_specs=in_specs, out_specs=out_specs, check_vma=False
    )
```

time: 1260 us -> 66.3 us (0.05)
  blocking collectives: 610 us -> 0 us
  waiting for transfers between devices: 490 us -> 0 us
  local copies, waits for them, and re-layouts: 71.6 us -> 0 us
  Pallas kernels: 0 us -> 65.5 us
  matrix products: 37.8 us -> 0 us
  starting transfers between devices: 23.4 us -> 0 us
  other arithmetic: 15.2 us -> 0 us
  between operations: 15.1 us -> 0.64 us
    unnamed x1 -> x0, blocking collectives: 583 us -> none
    psum x2 -> x0, waiting for transfers between devices: 490 us -> none  [the longest x1 408 us: on_device(): grad_gain, grad_table = lax.psum((grad_gain, grad_table), 'lon')]
    pallas_call x0 -> x2, Pallas kernels: none -> 65.5 us  [the longest x1 63.7 us: window_call(): pl.pallas_call(window_kernel, out_shape=(jax.ShapeDtypeStruct(grid, bf16)...]
    dot_general x13 -> x0, matrix products: 37.8 us -> none  [the longest x1 13 us: fold_bias(): jnp.einsum('bhxucyvd,cdr->bhxyuvr', shaped, longitude_onehot(WIN_LON), pr...]
    reshape x2 -> x0, local copies, waits for them, and re-layouts: 31.9 us -> none  [window_grads(): scores = scores + expand_bias(bias_rows)[:, None]]
    another operation x4 -> x0, local copies, waits for them, and re-layouts: 31.7 us -> none
    psum x1 -> x0, blocking collectives: 26.6 us -> none  [on_device(): lax.psum(grad_gain.astype(jnp.bfloat16), 'lat').astype(jnp.float32)]
    ppermute x4 -> x0, starting transfers between devices: 23.2 us -> none  [from_behind(): return lax.ppermute(value, axis, pairs)]
  transfers between devices with their start and end apart: 6 -> 0, of which waited for: 2 -> 0; matrix products, arithmetic and copies ran while one was open for 8% -> 0% of each run, Pallas kernels for 0% -> 0%
where the time goes in v2:
time: 66.3 us; the launch traced here: 66.1 us
  Pallas kernels  65.5 us (99%)
    pallas_call x1, Pallas kernels, window_call(): pl.pallas_call(window_kernel, out_shape=(jax.ShapeDtypeStruct(grid, bf16)...  63.7 us
    pallas_call x1, Pallas kernels, finish_call(): pl.pallas_call(finish_kernel, out_shape=(jax.ShapeDtypeStruct((WIN_LAT, W...  1.77 us

profile of v2, /device:TPU:1, one launch (start us, length us, event | category | flops | bytes accessed | tf_op | source)
XLA Modules:
  0.0 66.1 jit_solution(7160142927802345527)
XLA Ops:
  0.6 63.7 %window_gradients.1 = (bf16[6,12,2,384]{3,2,1,0:T(2,128)(2,1)}, f32[80,128]{1,0:T(8,128)}, bf16[32,16,128]{2,1,0:T(8,128)(2,1)}) custom-call(bf16[6,12,2,384]{3,2,1,0:T(2,128)(2,1)} %bitcast.5, bf16[6,12,2,384]{3,2,1,0:T(2,128)(2,1)} %bitcast.6, f32[384]{0:T(512)} %gain_hbm.1, bf16[384,1152]{1,0:T(8,128)(2,1)} %win_hbm.1, bf16[384,384]{1,0:T(8,128)(2,1)} %wout_hbm.1, ...), custom_call_target="tpu_custom_call" | custom-call | tf_op jit(solution)/shard_map/window_gradients/pallas_call | solution.py:514
  64.3 1.8 %outputs.1 = (bf16[6,12,2,384]{3,2,1,0:T(2,128)(2,1)}, bf16[6,1152]{1,0:T(8,128)(2,1)}, bf16[6,384]{1,0:T(8,128)(2,1)}, f32[384]{0:T(512)}, f32[12,1,3312]{2,1,0:T(1,128)}) custom-call(bf16[6,12,2,384]{3,2,1,0:T(2,128)(2,1)} %get-tuple-element.13.field, f32[80,128]{1,0:T(8,128)} %get-tuple-element.14.rows, bf16[32,16,128]{2,1,0:T(8,128)(2,1)} %get-tuple-element.15.table), custom_call_target="tpu_custom_call" | custom-call | tf_op jit(solution)/shard_map/outputs/pallas_call | solution.py:594

commit v3 on v2

--- a/solution.py
+++ b/solution.py
@@ -25,7 +25,7 @@
 TOKENS = 512 * CELLS
 TABLE_TILES = 26
 GROUPS = 3
-KEEP = 80
+KEEP = (32, 16)
 SCATTER = WIN_LON * ROWS * 16
 
 norm_eps = 1e-05
@@ -181,13 +181,14 @@
     return jnp.concatenate([a, jnp.zeros((WIDE - CELLS, a.shape[1]), a.dtype)], axis=0)
 
 
-def keep_rows():
-    shape = (2 * KEEP, CELLS + 16)
+def keep_rows(pieces, rows):
+    shape = (4 * rows, pieces * 12 + (16 if pieces == 4 else 0))
     row, col = iota(shape, 0), iota(shape, 1)
-    half, w = row // KEEP, row % KEEP
-    own = (w // 6) * 12 + half * 6 + w % 6
-    gain = CELLS + HEADS + jnp.minimum(w - 72, 3)
-    return (col == jnp.where(w < 72, own, gain)).astype(bf16)
+    part, w = row // rows, row % rows
+    mine = pieces // 2 * 6
+    own = ((part % 2) * (pieces // 2) + w // 6) * 12 + (part // 2) * 6 + w % 6
+    gain = jnp.where((part % 2 == 0) & (w < mine + 3), pieces * 12 + w - mine, -1)
+    return (col == jnp.where(w < mine, own, gain if pieces == 4 else -1)).astype(bf16)
 
 
 FAR_FIRST = (10, 6, 9, 11, 14, 2, 8, 5, 7, 13, 15, 1, 3, 4, 12)
@@ -198,24 +199,24 @@
     field_out, rows_out, table_out,
     field_land, cot_land, gain_v, w_in, w_out, table, reg, sel, feat, tprime, regs, stage,
     qkv, normt, bias, probs, dsf, dpt, att, tabf, grad_rows, gwin,
-    sums, pair, mine, chips, tsums, tpair, tmine, tchips, plane_sums, pack, pack_land, owned, zland,
-    hi_land,
+    sums, pair, mine, chips, last_sums, last_pair, last_mine, last_chips, tsums, tpair, tmine, tchips,
+    pack, pack_land, owned, zland, last_pack, last_pack_land, last_owned, last_zland, hi_send, hi_land,
+    ds_s,
     load_sem, own_sem, halo_send, halo_recv, back_send, back_recv, core_send, core_recv, chip_send,
-    chip_recv, z_send, z_recv, zp_sem, hi_sem, tab_send, tab_recv, last_sem,
+    chip_recv, z_send, z_recv, quad_send, quad_recv, hi_sem, tab_send, tab_recv, last_sem,
 ):
     x, y, z, core = place()
     xy = x * 4 + y
-    z_hi, parity = z // 8, z % 2
-    z_pair = z + 1 - 2 * parity
+    z_hi, member = z // 8, z % 4
     other_core = at(x, y, z, 1 - core)
 
     def plane(k):
         tx, ty = (x + k // 4) % 4, (y + k % 4) % 4
         return tx * 4 + ty, at(tx, ty, z, core)
 
-    partners = halo_partners() + [other_core]
-    partners += [plane(k)[1] for k in range(1, CHIPS)]
-    partners += [at(x, y, (z + k) % 16, core) for k in range(1, 16)]
+    partners = halo_partners()
+    partners += [at(x, y, (z + k) % 16, core) for k in (8, 7, 9, 6, 10, 5, 11, 4, 12, 3, 13, 2, 14, 1, 15)]
+    partners += [plane(k)[1] for k in FAR_FIRST] + [other_core]
     count = greet(partners)
     owns = [
         pltpu.make_async_copy(cells_part(src, 0, 0), window_part(dst, 0, 0), own_sem.at[i])
@@ -244,7 +245,8 @@
                     halo_recv.at[i, quad], window_owner(ha, ho, -1),
                 )
             )
-            halos[i][-1].start()
+    for copy in halos[0]:
+        copy.start()
     for copy in loads:
         copy.wait()
     same = same_region(reg, regs) > 0.5
@@ -253,6 +255,8 @@
     owns[0].wait()
     for copy in halos[0]:
         copy.wait_recv()
+    for copy in halos[1]:
+        copy.start()
     cells_to_rows(field_land, stage)
     cells = stage[...]
     centred = cells - jnp.mean(cells, axis=1, keepdims=True)
@@ -290,7 +294,7 @@
             p = s * (1.0 / jnp.sum(s, axis=1, keepdims=True))
             probs[h] = p
             att[h * 32 : h * 32 + 32, :] = nt(v_t[r : r + 32], p.astype(bf16)).astype(bf16)
-    att_t = nn(feat[1], att[...]).astype(bf16)
+    att_t = [nn(feat[i], att[...]).astype(bf16) for i in range(2)]
 
     owns[1].wait()
     for copy in halos[1]:
@@ -299,35 +303,60 @@
     cot = grad_rows[...].astype(bf16)
     qkv[:, 3 * D :] = nt(cot, w_out[...]).astype(bf16)
 
-    core_copies = [
-        remote(sums.at[g, 1 - core], pair.at[g], core_send.at[g], core_recv.at[g], other_core)
-        for g in range(GROUPS)
-    ]
-    core_copies.append(
-        remote(tsums.at[1 - core], tpair, core_send.at[3], core_recv.at[3], other_core)
-    )
+    def step_refs(g):
+        if g < 2:
+            return sums.at[g], pair.at[g], mine.at[g], chips.at[g]
+        if g == 2:
+            return last_sums, last_pair, last_mine, last_chips
+        return tsums, tpair, tmine, tchips
+
+    core_copies = []
+    for g in range(4):
+        src, dst = step_refs(g)[:2]
+        core_copies.append(
+            remote(src.at[1 - core], dst, core_send.at[g], core_recv.at[g], other_core)
+        )
     sends = [[], [], [], []]
 
     def to_plane(g):
         core_copies[g].wait_recv()
-        if g < GROUPS:
-            mine[g] = (sums[g, core].astype(f32) + pair[g].astype(f32)).astype(bf16)
-        else:
-            tmine[...] = (tsums[core].astype(f32) + tpair[...].astype(f32)).astype(bf16)
+        src, swapped, both, land = step_refs(g)
+        both[...] = (src.at[core][...].astype(f32) + swapped[...].astype(f32)).astype(bf16)
         for k in FAR_FIRST:
             index, device = plane(k)
-            src, dst = (
-                (mine.at[g, index], chips.at[g, k])
-                if g < GROUPS
-                else (tmine.at[index], tchips.at[k])
+            sends[g].append(
+                remote(both.at[index], land.at[k], chip_send.at[g, k], chip_recv.at[g, k], device)
             )
-            sends[g].append(remote(src, dst, chip_send.at[g, k], chip_recv.at[g, k], device))
             sends[g][-1].start()
 
-    for g in range(GROUPS):
-        q, k, v, do = part(0, g), pad_cells(part(1, g)), pad_cells(part(2, g)), part(3, g)
-        q_t = nt(eye, q).astype(bf16)
-        k_t = nt(eye, k).astype(bf16)
+    def from_plane(g):
+        _, _, both, land = step_refs(g)
+        for copy in sends[g]:
+            copy.wait_recv()
+        acc = both.at[xy][...].astype(f32)
+        for k in range(1, CHIPS):
+            acc = acc + land.at[k][...].astype(f32)
+        return acc.astype(bf16)
+
+    def pairs(blocks):
+        out = []
+        for even, odd in zip(blocks[::2], blocks[1::2]):
+            even, odd = even.reshape(32, 2, 8, 128), odd.reshape(32, 2, 8, 128)
+            out += [even[:, 0], even[:, 1] + odd[:, 0], odd[:, 1]]
+        return out
+
+    def put_sums(g, blocks):
+        sums[g] = (
+            jnp.concatenate(pairs(blocks), axis=1).astype(bf16).reshape(2, CHIPS, 48, 128)
+        )
+        core_copies[g].start()
+
+    def weight_block(which, g, odd):
+        lo = which * D + g * 128
+        return nt(normt[odd], dpt[lo : lo + 128, :])
+
+    def grad_scores(g):
+        v, do = pad_cells(part(2, g)), part(3, g)
         do_t = nt(eye, do).astype(bf16)
         grad_probs = nt(four_heads(do), v)
         for e in range(4):
@@ -335,45 +364,86 @@
             r = e * HEAD_DIM
             p = probs[h]
             dp = grad_probs[e * CELLS : (e + 1) * CELLS]
+            ds = p * (dp - jnp.sum(p * dp, axis=1, keepdims=True))
+            put_head_rows(dsf, h, ds)
+            ds_s[h] = (ds * scale).astype(bf16)
             dpt[2 * D + h * 32 : 2 * D + h * 32 + 32, :] = nn(do_t[r : r + 32], p.astype(bf16))[
                 :, :CELLS
             ].astype(bf16)
-            ds = p * (dp - jnp.sum(p * dp, axis=1, keepdims=True))
-            put_head_rows(dsf, h, ds)
-            ds_low = (ds * scale).astype(bf16)
+
+    out_blocks = [nn(att_t[g % 2], cot[:, g * 128 : g * 128 + 128]) for g in range(GROUPS)]
+    grad_scores(0)
+    put_sums(0, out_blocks + [weight_block(2, 0, 1)])
+    grad_scores(1)
+    grad_scores(2)
+
+    def grad_heads(g):
+        q_t = nt(eye, part(0, g)).astype(bf16)
+        k_t = nt(eye, pad_cells(part(1, g))).astype(bf16)
+        for e in range(4):
+            h = g * 4 + e
+            r = e * HEAD_DIM
+            ds_low = ds_s[h]
             dpt[h * 32 : h * 32 + 32, :] = nt(k_t[r : r + 32], ds_low).astype(bf16)
             dpt[D + h * 32 : D + h * 32 + 32, :] = nn(q_t[r : r + 32], ds_low)[:, :CELLS].astype(
                 bf16
             )
-        blocks = [
-            nt(normt[which % 2], dpt[which * D + g * 128 : which * D + g * 128 + 128, :])
-            for which in range(3)
-        ]
-        blocks.append(nn(att_t, cot[:, g * 128 : g * 128 + 128]))
-        b0, b1, b2, b3 = (b.reshape(32, 2, 8, 128) for b in blocks)
-        sums[g] = (
-            jnp.concatenate(
-                [b0[:, 0], b0[:, 1] + b1[:, 0], b1[:, 1], b2[:, 0], b2[:, 1] + b3[:, 0], b3[:, 1]],
-                axis=1,
-            )
-            .astype(bf16)
-            .reshape(2, CHIPS, 48, 128)
+
+    grad_heads(0)
+    put_sums(
+        1,
+        [weight_block(2, 1, 0), weight_block(2, 2, 1), weight_block(0, 0, 0), weight_block(1, 0, 1)],
+    )
+    to_plane(0)
+
+    acc = jnp.zeros((192, 2 * HALF_POS), f32)
+    for c in range(WIN_LON):
+        rows = jnp.concatenate(
+            [dsf[pl.ds(half * SCATTER + c * 192, 192), :] for half in range(2)], axis=1
         )
-        core_copies[g].start()
-        if g:
-            to_plane(g - 1)
+        acc = acc + nt(rows.astype(bf16), sel[c])
+    tabf[:, 25 * 128 : 32 * 128] = jnp.zeros((16, 7 * 128), f32)
+    for row in range(ROWS):
+        for half in range(2):
+            off = table_offset(row, half)
+            tabf[:, off : off + HALF_POS] = acc[
+                row * 16 : row * 16 + 16, half * HALF_POS : (half + 1) * HALF_POS
+            ]
+    for t in range(32):
+        tsums[t // 16, t % 16] = tabf[:, t * 128 : t * 128 + 128].astype(bf16)
+    core_copies[3].start()
+    to_plane(1)
+
+    grad_heads(1)
+    grad_heads(2)
 
     shifted_t = nn(w_in[...], dpt[...]).astype(bf16)
     eye_c = (iota((CELLS, CELLS), 0) == iota((CELLS, CELLS), 1)).astype(bf16)
     g_normed = nt(eye_c, shifted_t)
     normalized = stage[...]
+    grad_gain = jnp.sum(g_normed * normalized, axis=0, keepdims=True)
+    extra = jnp.concatenate(
+        [grad_gain[:, k * 128 : k * 128 + 128] for k in range(3)] + [jnp.zeros((13, 128), f32)],
+        axis=0,
+    )
+    last_sums[...] = (
+        jnp.concatenate(
+            pairs([weight_block(i % 2, 1 + i // 2, i % 2) for i in range(4)])
+            + [jnp.broadcast_to(extra[None], (32, 16, 128))],
+            axis=1,
+        )
+        .astype(bf16)
+        .reshape(2, CHIPS, 64, 128)
+    )
+    core_copies[2].start()
+    to_plane(3)
     scaled = g_normed * gain
-    grad_gain = jnp.sum(g_normed * normalized, axis=0, keepdims=True)
     grad_rows[...] = cot.astype(f32) + inv_std * (
         scaled
         - jnp.mean(scaled, axis=1, keepdims=True)
         - normalized * jnp.mean(scaled * normalized, axis=1, keepdims=True)
     )
+    to_plane(2)
     for a in range(WIN_LAT):
         for o in range(WIN_LON):
             p = o * ROWS + a * 2
@@ -388,85 +458,86 @@
             )
         )
         backs[-1].start()
-    to_plane(2)
-
-    for h in range(HEADS, 16):
-        put_head_rows(dsf, h, jnp.zeros((CELLS, WIDE), f32))
-    acc = jnp.zeros((192, 2 * HALF_POS), f32)
-    for c in range(WIN_LON):
-        rows = jnp.concatenate(
-            [dsf[pl.ds(half * SCATTER + c * 192, 192), :] for half in range(2)], axis=1
-        )
-        acc = acc + nt(rows.astype(bf16), sel[c])
-    tabf[:, 25 * 128 : 32 * 128] = jnp.zeros((16, 7 * 128), f32)
-    for row in range(ROWS):
-        for half in range(2):
-            off = table_offset(row, half)
-            tabf[:, off : off + HALF_POS] = acc[
-                row * 16 : row * 16 + 16, half * HALF_POS : (half + 1) * HALF_POS
-            ]
-    spare = jnp.concatenate(
-        [grad_gain[:, k * 128 : k * 128 + 128] for k in range(3)] + [jnp.zeros((1, 128), f32)],
-        axis=0,
-    )
-    for t in range(32):
-        tsums[t // 16, t % 16] = jnp.concatenate(
-            [tabf[0:HEADS, t * 128 : t * 128 + 128], spare], axis=0
-        ).astype(bf16)
-    core_copies[3].start()
+    hi_send[...] = from_plane(3)
+    hi = remote(hi_send, hi_land, hi_sem.at[0], hi_sem.at[1], at(x, y, (z + 8) % 16, core))
+    hi.start()
     for a in range(3):
         for o in range(6):
             field_out[3 + a, 6 + o] = gwin[a, o]
-    to_plane(3)
-
-    for g in range(GROUPS):
-        for copy in sends[g]:
-            copy.wait_recv()
-        acc = mine[g, xy].astype(f32)
-        for k in range(1, CHIPS):
-            acc = acc + chips[g, k].astype(f32)
-        plane_sums[g * 48 : (g + 1) * 48, :] = acc.astype(bf16)
-    for copy in sends[3]:
-        copy.wait_recv()
-    acc = tmine[xy].astype(f32)
-    for k in range(1, CHIPS):
-        acc = acc + tchips[k].astype(f32)
-    plane_sums[CELLS : CELLS + 16, :] = acc.astype(bf16)
-
-    pack[...] = nn(keep_rows(), plane_sums[...]).astype(bf16).reshape(2, KEEP, 128)
-    swap = remote(
-        pack.at[1 - parity], pack_land, zp_sem.at[0], zp_sem.at[1], at(x, y, z_pair, core)
-    )
-    swap.start()
-    table_part = plane_sums.at[pl.ds(CELLS, 16)]
-    hi = remote(table_part, hi_land, hi_sem.at[0], hi_sem.at[1], at(x, y, (z + 8) % 16, core))
-    hi.start()
-    swap.wait_recv()
-    owned[...] = (pack[parity].astype(f32) + pack_land[...].astype(f32)).astype(bf16)
+
+    my_part = (z // 4) * 2 + member % 2
 
     def keeper(j):
-        return parity * 8 + (z + 4 + j) % 8
-
-    def to_keeper(j):
+        return (member // 2) * 8 + (z + 4 + j) % 8
+
+    def z_refs(i):
+        if i == 0:
+            return pack, pack_land, owned, zland
+        return last_pack, last_pack_land, last_owned, last_zland
+
+    def to_four(i, select, rows):
+        packed, land = z_refs(i)[:2]
+        packed[...] = nn(select, rows).astype(bf16).reshape(4, KEEP[i], 128)
+        copies = []
+        for k in range(1, 4):
+            to = (member + k) % 4
+            copies.append(
+                remote(
+                    packed.at[to], land.at[k], quad_send.at[i, k], quad_recv.at[i, k],
+                    at(x, y, z - member + to, core),
+                )
+            )
+            copies[-1].start()
+        return copies
+
+    def to_keeper(i, j):
+        _, _, mine_z, land = z_refs(i)
         return remote(
-            owned, zland.at[z // 2], z_send.at[j], z_recv.at[z // 2], at(x, y, keeper(j), core)
+            mine_z, land.at[my_part], z_send.at[i, j], z_recv.at[i, my_part],
+            at(x, y, keeper(j), core),
         )
 
-    for j in range(8):
-
-        @pl.when(keeper(j) != z)
-        def _(j=j):
-            to_keeper(j).start()
-
-    @pl.when(parity == z_hi)
-    def _():
-        zland[z // 2] = owned[...]
+    def to_keepers(i, copies):
+        packed, four, mine_z, land = z_refs(i)
+        acc = packed.at[member][...].astype(f32)
+        for k in range(1, 4):
+            copies[k - 1].wait_recv()
+            acc = acc + four[k].astype(f32)
+        mine_z[...] = acc.astype(bf16)
+        for j in range(8):
+
+            @pl.when(keeper(j) != z)
+            def _(j=j):
+                to_keeper(i, j).start()
+
+        @pl.when(member // 2 == z_hi)
+        def _():
+            land[my_part] = mine_z[...]
+
+    def kept(i):
+        _, _, mine_z, land = z_refs(i)
+        for s in range(8):
+
+            @pl.when((s // 2) * 4 + 2 * z_hi + s % 2 != z)
+            def _(s=s):
+                remote(mine_z, land.at[s], z_send.at[i, 0], z_recv.at[i, s], other_core).wait_recv()
+
+        lo = i * KEEP[0]
+        for half in range(2):
+            total = land[half].astype(f32)
+            for k in range(1, 4):
+                total = total + land[2 * k + half].astype(f32)
+            rows_out[half, lo : lo + KEEP[i]] = total
+
+    selects = [keep_rows(8, KEEP[0]), keep_rows(4, KEEP[1])]
+    quads = to_four(0, selects[0], jnp.concatenate([from_plane(0), from_plane(1)], axis=0))
+    last_quads = to_four(1, selects[1], from_plane(2))
+    to_keepers(0, quads)
+    to_keepers(1, last_quads)
 
     hi.wait_recv()
     slot = core * CHIPS + xy
-    table_out[slot] = (plane_sums[CELLS : CELLS + 16].astype(f32) + hi_land[...].astype(f32)).astype(
-        bf16
-    )
+    table_out[slot] = (hi_send[...].astype(f32) + hi_land[...].astype(f32)).astype(bf16)
     tab_copies = []
     for k in FAR_FIRST:
         tab_copies.append(
@@ -476,35 +547,26 @@
         )
         tab_copies[-1].start()
 
-    for i in range(8):
-
-        @pl.when(2 * i + z_hi != z)
-        def _(i=i):
-            remote(
-                owned, zland.at[i], z_send.at[0], z_recv.at[i], at(x, y, z_pair, core)
-            ).wait_recv()
-
-    total = zland[0].astype(f32)
-    for i in range(1, 8):
-        total = total + zland[i].astype(f32)
-    rows_out[...] = total
-
     for copy in tab_copies:
         copy.wait_recv()
     half = table_out.at[pl.ds(core * CHIPS, CHIPS)]
     last = remote(half, half, last_sem.at[0], last_sem.at[1], other_core)
     last.start()
-    for copy in backs + [last]:
+    for copy in backs:
         copy.wait_recv()
-    for copy in halos[0] + halos[1] + core_copies + sum(sends, []) + backs + [swap, hi, last]:
+    kept(0)
+    kept(1)
+    last.wait_recv()
+    for copy in halos[0] + halos[1] + core_copies + sum(sends, []) + backs + quads + last_quads:
         copy.wait_send()
-    for copy in tab_copies:
+    for copy in tab_copies + [hi, last]:
         copy.wait_send()
-    for j in range(8):
-
-        @pl.when(keeper(j) != z)
-        def _(j=j):
-            to_keeper(j).wait_send()
+    for i in range(2):
+        for j in range(8):
+
+            @pl.when(keeper(j) != z)
+            def _(i=i, j=j):
+                to_keeper(i, j).wait_send()
 
 
 def window_call(*args):
@@ -515,7 +577,7 @@
         window_kernel,
         out_shape=(
             jax.ShapeDtypeStruct(grid, bf16),
-            jax.ShapeDtypeStruct((KEEP, 128), f32),
+            jax.ShapeDtypeStruct((2, KEEP[0] + KEEP[1], 128), f32),
             jax.ShapeDtypeStruct((32,) + tile, bf16),
         ),
         in_specs=[pl.BlockSpec(memory_space=pl.ANY)] * 9,
@@ -543,23 +605,32 @@
             VMEM((16, 32 * 128), f32),
             VMEM((CELLS, D), f32),
             VMEM(grid, bf16),
-            VMEM((GROUPS, 2, CHIPS, 48, 128), bf16),
-            VMEM((GROUPS, CHIPS, 48, 128), bf16),
-            VMEM((GROUPS, CHIPS, 48, 128), bf16),
-            VMEM((GROUPS, CHIPS, 48, 128), bf16),
+            VMEM((2, 2, CHIPS, 48, 128), bf16),
+            VMEM((2, CHIPS, 48, 128), bf16),
+            VMEM((2, CHIPS, 48, 128), bf16),
+            VMEM((2, CHIPS, 48, 128), bf16),
+            VMEM((2, CHIPS, 64, 128), bf16),
+            VMEM((CHIPS, 64, 128), bf16),
+            VMEM((CHIPS, 64, 128), bf16),
+            VMEM((CHIPS, 64, 128), bf16),
             VMEM((2, CHIPS) + tile, bf16),
             VMEM((CHIPS,) + tile, bf16),
             VMEM((CHIPS,) + tile, bf16),
             VMEM((CHIPS,) + tile, bf16),
-            VMEM((CELLS + 16, 128), bf16),
-            VMEM((2, KEEP, 128), bf16),
-            VMEM((KEEP, 128), bf16),
-            VMEM((KEEP, 128), bf16),
-            VMEM((8, KEEP, 128), bf16),
+            VMEM((4, KEEP[0], 128), bf16),
+            VMEM((4, KEEP[0], 128), bf16),
+            VMEM((KEEP[0], 128), bf16),
+            VMEM((8, KEEP[0], 128), bf16),
+            VMEM((4, KEEP[1], 128), bf16),
+            VMEM((4, KEEP[1], 128), bf16),
+            VMEM((KEEP[1], 128), bf16),
+            VMEM((8, KEEP[1], 128), bf16),
             VMEM(tile, bf16),
+            VMEM(tile, bf16),
+            VMEM((HEADS, CELLS, WIDE), bf16),
             sem((7,)), sem((2,)), sem((2, 4)), sem((2, 4)), sem((4,)), sem((4,)), sem((4,)),
-            sem((4,)), sem((4, CHIPS)), sem((4, CHIPS)), sem((8,)), sem((8,)), sem((2,)),
-            sem((2,)), sem((CHIPS,)), sem((CHIPS,)), sem((2,)),
+            sem((4,)), sem((4, CHIPS)), sem((4, CHIPS)), sem((2, 8)), sem((2, 8)),
+            sem((2, 4)), sem((2, 4)), sem((2,)), sem((CHIPS,)), sem((CHIPS,)), sem((2,)),
         ],
         compiler_params=pltpu.CompilerParams(
             collective_id=0, has_side_effects=True, vmem_limit_bytes=60 * 1024 * 1024
@@ -568,21 +639,25 @@
     )(*args)
 
 
+PIECES = (
+    (3, 0), (3, 1), (3, 2), (2, 0), (2, 1), (2, 2), (0, 0), (1, 0), (0, 1), (1, 1), (0, 2), (1, 2),
+)
+
+
 def finish_kernel(field, rows, table, out_field, out_win, out_wout, out_gain, out_table):
     factor = 1.0 / math.sqrt(TOKENS)
     out_field[...] = field[...]
     sums = rows[...] * factor
-    for g in range(GROUPS):
-        for which in range(4):
-            at_row = (g * 4 + which) * 6
-            part = sums[at_row : at_row + 6].astype(bf16)
-            if which < 3:
-                lo = which * D + g * 128
-                out_win[:, lo : lo + 128] = part
-            else:
-                out_wout[:, g * 128 : g * 128 + 128] = part
+    for i, (which, g) in enumerate(PIECES):
+        half, at_row = (i // 4, (i % 4) * 6) if i < 8 else ((i - 8) // 2, KEEP[0] + (i % 2) * 6)
+        part = sums[half, at_row : at_row + 6].astype(bf16)
+        if which < 3:
+            lo = which * D + g * 128
+            out_win[:, lo : lo + 128] = part
+        else:
+            out_wout[:, g * 128 : g * 128 + 128] = part
     for k in range(3):
-        out_gain[k * 128 : k * 128 + 128] = sums[72 + k]
+        out_gain[k * 128 : k * 128 + 128] = sums[0, KEEP[0] + 12 + k]
     for t in range(TABLE_TILES):
         width = min(128, POS - t * 128)
         values = table[t].astype(f32)

time: 66.3 us -> 63.1 us (0.952)
  Pallas kernels: 65.5 us -> 62.3 us
    pallas_call x1, Pallas kernels: 63.7 us -> 60.6 us  [window_call(): pl.pallas_call(window_kernel, out_shape=(jax.ShapeDtypeStruct(grid, bf16)...]
where the time goes in v3:
time: 63.1 us; the launch traced here: 63 us
  Pallas kernels  62.3 us (99%)
  between operations  0.64 us (1%)
    pallas_call x1, Pallas kernels, window_call(): pl.pallas_call(window_kernel, out_shape=(jax.ShapeDtypeStruct(grid, bf16)...  60.6 us
    pallas_call x1, Pallas kernels, finish_call(): pl.pallas_call(finish_kernel, out_shape=(jax.ShapeDtypeStruct((WIN_LAT, W...  1.78 us

profile of v3, /device:TPU:1, one launch (start us, length us, event | category | flops | bytes accessed | tf_op | source)
XLA Modules:
  0.0 63.0 jit_solution(10635023145742745864)
XLA Ops:
  0.6 60.6 %window_gradients.1 = (bf16[6,12,2,384]{3,2,1,0:T(2,128)(2,1)}, f32[2,48,128]{2,1,0:T(8,128)}, bf16[32,16,128]{2,1,0:T(8,128)(2,1)}) custom-call(bf16[6,12,2,384]{3,2,1,0:T(2,128)(2,1)} %bitcast.5, bf16[6,12,2,384]{3,2,1,0:T(2,128)(2,1)} %bitcast.6, f32[384]{0:T(512)} %gain_hbm.1, bf16[384,1152]{1,0:T(8,128)(2,1)} %win_hbm.1, bf16[384,384]{1,0:T(8,128)(2,1)} %wout_hbm.1, ...), custom_call_target="tpu_custom_call" | custom-call | tf_op jit(solution)/shard_map/window_gradients/pallas_call | solution.py:576
  61.2 1.8 %outputs.1 = (bf16[6,12,2,384]{3,2,1,0:T(2,128)(2,1)}, bf16[6,1152]{1,0:T(8,128)(2,1)}, bf16[6,384]{1,0:T(8,128)(2,1)}, f32[384]{0:T(512)}, f32[12,1,3312]{2,1,0:T(1,128)}) custom-call(bf16[6,12,2,384]{3,2,1,0:T(2,128)(2,1)} %get-tuple-element.13.field, f32[2,48,128]{2,1,0:T(8,128)} %get-tuple-element.14.rows, bf16[32,16,128]{2,1,0:T(8,128)(2,1)} %get-tuple-element.15.table), custom_call_target="tpu_custom_call" | custom-call | tf_op jit(solution)/shard_map/outputs/pallas_call | solution.py:669

commit v4 on v3

--- a/solution.py
+++ b/solution.py
@@ -26,7 +26,7 @@
 TABLE_TILES = 26
 GROUPS = 3
 KEEP = (32, 16)
-SCATTER = WIN_LON * ROWS * 16
+SCATTER = WIN_LON * ROWS * HEADS
 
 norm_eps = 1e-05
 masked_score = -1000000000.0
@@ -65,13 +65,13 @@
 
 def head_rows(ref, h):
     return jnp.concatenate(
-        [ref[pl.ds(half * SCATTER + h, CELLS, stride=16), :] for half in range(2)], axis=1
+        [ref[pl.ds(half * SCATTER + h, CELLS, stride=HEADS), :] for half in range(2)], axis=1
     )
 
 
 def put_head_rows(ref, h, value):
     for half in range(2):
-        ref[pl.ds(half * SCATTER + h, CELLS, stride=16), :] = value[:, half * 128 : half * 128 + 128]
+        ref[pl.ds(half * SCATTER + h, CELLS, stride=HEADS), :] = value[:, half * 128 : half * 128 + 128]
 
 
 def nt(a, b):
@@ -144,15 +144,15 @@
     for row in range(ROWS):
         for y in range(2):
             off = table_offset(row, y)
-            tprime[row * 16 : row * 16 + HEADS, y * HALF_POS : (y + 1) * HALF_POS] = table[
+            tprime[row * HEADS : (row + 1) * HEADS, y * HALF_POS : (y + 1) * HALF_POS] = table[
                 :, off : off + HALF_POS
             ]
     rows = tprime[...].astype(bf16)
     for c in range(WIN_LON):
         part = nn(rows, sel_ref[c])
         for half in range(2):
-            base = half * SCATTER + c * 192
-            bias[base : base + 192, :] = part[:, half * 128 : half * 128 + 128]
+            base = half * SCATTER + c * CELLS
+            bias[base : base + CELLS, :] = part[:, half * 128 : half * 128 + 128]
 
 
 def same_region(reg, regs):
@@ -396,18 +396,18 @@
     )
     to_plane(0)
 
-    acc = jnp.zeros((192, 2 * HALF_POS), f32)
+    acc = jnp.zeros((CELLS, 2 * HALF_POS), f32)
     for c in range(WIN_LON):
         rows = jnp.concatenate(
-            [dsf[pl.ds(half * SCATTER + c * 192, 192), :] for half in range(2)], axis=1
+            [dsf[pl.ds(half * SCATTER + c * CELLS, CELLS), :] for half in range(2)], axis=1
         )
         acc = acc + nt(rows.astype(bf16), sel[c])
-    tabf[:, 25 * 128 : 32 * 128] = jnp.zeros((16, 7 * 128), f32)
+    tabf[...] = jnp.zeros_like(tabf)
     for row in range(ROWS):
         for half in range(2):
             off = table_offset(row, half)
-            tabf[:, off : off + HALF_POS] = acc[
-                row * 16 : row * 16 + 16, half * HALF_POS : (half + 1) * HALF_POS
+            tabf[0:HEADS, off : off + HALF_POS] = acc[
+                row * HEADS : (row + 1) * HEADS, half * HALF_POS : (half + 1) * HALF_POS
             ]
     for t in range(32):
         tsums[t // 16, t % 16] = tabf[:, t * 128 : t * 128 + 128].astype(bf16)
@@ -592,7 +592,7 @@
             VMEM((WIN_LAT, LEV, WIN_LON), jnp.int32),
             VMEM((WIN_LON, 2 * HALF_POS, WIDE), bf16),
             VMEM((2, 512, D), bf16),
-            VMEM((192, 2 * HALF_POS), f32),
+            VMEM((CELLS, 2 * HALF_POS), f32),
             VMEM((16, 128), f32),
             VMEM((CELLS, D), f32),
             VMEM((CELLS, 4 * D), bf16),

time: 63.1 us -> 63.2 us (level)
  no operation moved by 1% of the time
where the time goes in v4:
time: 63.2 us; the launch traced here: 63.1 us
  Pallas kernels  62.4 us (99%)
  between operations  0.64 us (1%)
    pallas_call x1, Pallas kernels, window_call(): pl.pallas_call(window_kernel, out_shape=(jax.ShapeDtypeStruct(grid, bf16)...  60.7 us
    pallas_call x1, Pallas kernels, finish_call(): pl.pallas_call(finish_kernel, out_shape=(jax.ShapeDtypeStruct((WIN_LAT, W...  1.78 us

profile of v4, /device:TPU:1, one launch (start us, length us, event | category | flops | bytes accessed | tf_op | source)
XLA Modules:
  0.0 63.1 jit_solution(13813081672823654165)
XLA Ops:
  0.6 60.7 %window_gradients.1 = (bf16[6,12,2,384]{3,2,1,0:T(2,128)(2,1)}, f32[2,48,128]{2,1,0:T(8,128)}, bf16[32,16,128]{2,1,0:T(8,128)(2,1)}) custom-call(bf16[6,12,2,384]{3,2,1,0:T(2,128)(2,1)} %bitcast.5, bf16[6,12,2,384]{3,2,1,0:T(2,128)(2,1)} %bitcast.6, f32[384]{0:T(512)} %gain_hbm.1, bf16[384,1152]{1,0:T(8,128)(2,1)} %win_hbm.1, bf16[384,384]{1,0:T(8,128)(2,1)} %wout_hbm.1, ...), custom_call_target="tpu_custom_call" | custom-call | tf_op jit(solution)/shard_map/window_gradients/pallas_call | solution.py:576
  61.3 1.8 %outputs.1 = (bf16[6,12,2,384]{3,2,1,0:T(2,128)(2,1)}, bf16[6,1152]{1,0:T(8,128)(2,1)}, bf16[6,384]{1,0:T(8,128)(2,1)}, f32[384]{0:T(512)}, f32[12,1,3312]{2,1,0:T(1,128)}) custom-call(bf16[6,12,2,384]{3,2,1,0:T(2,128)(2,1)} %get-tuple-element.13.field, f32[2,48,128]{2,1,0:T(8,128)} %get-tuple-element.14.rows, bf16[32,16,128]{2,1,0:T(8,128)(2,1)} %get-tuple-element.15.table), custom_call_target="tpu_custom_call" | custom-call | tf_op jit(solution)/shard_map/outputs/pallas_call | solution.py:669
